TPU v7x, 512 devices: a whole 4x8x8 slice. The times are simulated.
512 devices in a mesh: dp: 64 (over z, x, core), fsdp: 8 (over y).
Axes of the slice: x: 4, y: 8, z: 8, core: 2. Of those that a mesh axis runs over, the one named last changes fastest.
Arguments:
- waveform: float32 [4096, 400], P(('dp', 'fsdp')), may hold values from -6 to 6
- lengths: int32 [4096], P(('dp', 'fsdp')), may hold values from 200 to 400, as said below
- owner_of: int32 [4096], P(('dp', 'fsdp')), may hold values from 0 to 63, as said below
- targets: float32 [4096, 39], P(('dp', 'fsdp')), may hold values from -5 to 5
- first_weight: float32 [10, 512], replicated, may hold values from -2 to 2
- first_gain: float32 [512], replicated, may hold values from 0.1 to 1.9
- first_shift: float32 [512], replicated, may hold values from -3 to 3
- second_weight: bfloat16 [1536, 512], P('fsdp'), may hold values from -0.15625 to 0.15625
- second_gain: float32 [512], replicated, may hold values from 0.1 to 1.9
- second_shift: float32 [512], replicated, may hold values from -3 to 3
Outputs:
- logvar: float32 [4096, 39], P(('dp', 'fsdp'))
- loss: float32 [], replicated
- grad_second_weight: float32 [1536, 512], P('fsdp')
- grad_first_weight: float32 [10, 512], replicated
- grad_first_gain: float32 [512], replicated
- grad_first_shift: float32 [512], replicated
- grad_second_gain: float32 [512], replicated
- grad_second_shift: float32 [512], replicated
Inputs may be any that keep to these rules, and one draw needn't show every extreme that they name: `lengths`: every draw has a row of length 400 and one of length 200. `owner_of`: rows read by the devices of one fsdp index go to owners of the same fsdp index. From one reader, each owner receives either no row or exactly 1 row; every owner receives exactly 8 rows.
All inputs are finite; a program needn't handle non-finite values.
Results may differ from a plain program's by a relative error of at most 0.0019.
Values may be sent and summed in bfloat16 or wider, within the bound.
A program may use at most 64 MiB of HBM per device.

v0:
```python
import functools
import math

import jax
import jax.numpy as jnp
from jax import lax
from jax.sharding import Mesh
from jax.sharding import PartitionSpec as P

DP = ("dp_0", "dp_1", "dp_2")
DP_FSDP = ("dp_0", "dp_1", "dp_2", "fsdp")


epsilon = 1e-05


def side_by_side(arrays, axis, split_dim, concat_dim, along):
    widths = [math.prod(a.shape[along:]) for a in arrays]
    both = jnp.concatenate(
        [a.reshape(*a.shape[:along], w) for a, w in zip(arrays, widths)], axis=along
    )
    whole = lax.all_to_all(both, axis, split_axis=split_dim, concat_axis=concat_dim, tiled=True)
    pieces = jnp.split(whole, [sum(widths[:k]) for k in range(1, len(widths))], axis=along)
    return tuple(
        (b.reshape(*whole.shape[:along], *a.shape[along:]) for a, b in zip(arrays, pieces))
    )


def in_order(pieces, dim):
    shape = list(pieces.shape[1:])
    shape[dim] *= pieces.shape[0]
    return jnp.moveaxis(pieces, 0, dim).reshape(shape)


def copy_for_each(array, axis):
    copies = jnp.broadcast_to(array, (lax.axis_size(axis), *array.shape))
    return lax.all_to_all(copies, axis, split_axis=0, concat_axis=0, tiled=True)


def gathered_copies(array, axis, dim):
    return in_order(copy_for_each(array, axis), dim)


def own_block(pieces, axes, turns):
    shape = [lax.axis_size(a) for a in axes]
    pieces = pieces.reshape(*shape, *pieces.shape[1:])
    pieces = pieces.transpose(*turns, *range(len(axes), pieces.ndim))
    pieces = pieces.reshape(-1, *pieces.shape[len(axes) :])
    for k in turns:
        pieces = lax.psum_scatter(pieces, axes[k], scatter_dimension=0, tiled=True)
    return pieces[0]


def split_up(array, dim, peers):
    shape = array.shape
    pieces = array.reshape(*shape[:dim], peers, shape[dim] // peers, *shape[dim + 1 :])
    return jnp.moveaxis(pieces, dim, 0)


def summed_rows(array, axes, turns, dim):
    peers = lax.axis_size(axes)
    return own_block(split_up(array, dim, peers), axes, turns)


def one_axis_at_a_time(array, axes):
    return functools.reduce(lax.psum, axes, array)


def layer_norm(values, norm_gain, norm_shift):
    row_mean = jnp.mean(values, axis=-1, keepdims=True)
    centered = values - row_mean
    row_var = jnp.mean(centered * centered, axis=-1, keepdims=True)
    return centered * lax.rsqrt(row_var + epsilon) * norm_gain + norm_shift


def first_layer(waveform, first_weight, first_gain, first_shift):
    row_total, samples = waveform.shape
    frames = samples // 5 - 1
    blocks = waveform.reshape(row_total, samples // 5, 5)
    windows = jnp.concatenate([blocks[:, :frames], blocks[:, 1 : frames + 1]], axis=2)
    pre_norm = jnp.dot(
        windows.reshape(row_total * frames, 10),
        first_weight,
        precision=lax.Precision.HIGHEST,
        preferred_element_type=jnp.float32,
    )
    return jax.nn.gelu(layer_norm(pre_norm, first_gain, first_shift), approximate=False)


def make_patches(activated, row_total):
    channels = activated.shape[1]
    frames = activated.shape[0] // row_total
    later = (frames - 1) // 2
    shaped = activated.reshape(row_total, frames, channels)
    padded = jnp.concatenate([shaped, jnp.zeros((row_total, 1, channels), activated.dtype)], axis=1)
    paired = padded.reshape(row_total, later + 1, 2, channels)
    even_frames = paired[:, :, 0]
    odd_frames = paired[:, :, 1]
    joined = jnp.concatenate(
        [even_frames[:, :later], odd_frames[:, :later], even_frames[:, 1:]], axis=2
    )
    return joined.reshape(row_total * later, 3 * channels)


def patch_grad(grad_patches, row_total, frames):
    channels = grad_patches.shape[1] // 3
    later = grad_patches.shape[0] // row_total
    shaped = grad_patches.reshape(row_total, later, 3, channels)
    zero_frame = jnp.zeros((row_total, 1, channels), grad_patches.dtype)
    even_frames = jnp.concatenate([shaped[:, :, 0], zero_frame], axis=1) + jnp.concatenate(
        [zero_frame, shaped[:, :, 2]], axis=1
    )
    odd_frames = jnp.concatenate([shaped[:, :, 1], zero_frame], axis=1)
    paired = jnp.stack([even_frames, odd_frames], axis=2).reshape(
        row_total, 2 * later + 2, channels
    )
    return paired[:, :frames].reshape(row_total * frames, channels)


def frame_mask_of(row_lengths, later):
    first_valid = (row_lengths - 10) // 5 + 1
    second_valid = (first_valid - 3) // 2 + 1
    inside = jnp.arange(later, dtype=jnp.int32)[None, :] < second_valid[:, None]
    return inside.astype(jnp.float32).reshape(-1)


def head_loss(second_pre, second_gain, second_shift, target_flat, frame_mask):
    activated = jax.nn.gelu(layer_norm(second_pre, second_gain, second_shift), approximate=False)
    row_mean = jnp.mean(activated, axis=-1, keepdims=True)
    centered = activated - row_mean
    raw_logvar = jnp.log(jnp.mean(centered * centered, axis=-1) + epsilon)
    misfit = raw_logvar - target_flat
    return (jnp.sum(frame_mask * misfit * misfit), raw_logvar)


def per_device(
    waveform,
    lengths,
    owner_of,
    targets,
    first_weight,
    first_gain,
    first_shift,
    second_weight,
    second_gain,
    second_shift,
):
    peer_count = lax.axis_size(DP)
    row_total, samples = waveform.shape
    later = targets.shape[1]
    frames = samples // 5 - 1
    per_owner = max(1, 2 * row_total // peer_count)
    slot_count = peer_count * per_owner
    matches = (owner_of[:, None] == owner_of[None, :]).astype(jnp.int32)
    earlier = jnp.sum(jnp.tril(matches, -1), axis=1)
    slot_index = owner_of * per_owner + earlier
    placing = (slot_index[:, None] == jnp.arange(slot_count, dtype=jnp.int32)[None, :]).astype(
        jnp.float32
    )
    sent_wave = lax.dot_general(
        placing,
        waveform,
        (((0,), (0,)), ((), ())),
        precision=lax.Precision.HIGHEST,
        preferred_element_type=jnp.float32,
    )
    sent_length = jnp.dot(
        lengths.astype(jnp.float32),
        placing,
        precision=lax.Precision.HIGHEST,
        preferred_element_type=jnp.float32,
    )
    got_wave, got_length = side_by_side(
        (
            sent_wave.reshape(peer_count, per_owner, samples),
            sent_length.reshape(peer_count, per_owner),
        ),
        DP,
        0,
        0,
        2,
    )
    got_wave = got_wave.reshape(slot_count, samples)
    got_length = got_length.reshape(slot_count)
    present = got_length > 0.5
    arrival = jnp.cumsum(present.astype(jnp.int32)) - 1
    picking = (
        present[None, :] & (arrival[None, :] == jnp.arange(row_total, dtype=jnp.int32)[:, None])
    ).astype(jnp.float32)
    owned_wave = jnp.dot(
        picking, got_wave, precision=lax.Precision.HIGHEST, preferred_element_type=jnp.float32
    )
    owned_length = jnp.dot(
        picking, got_length, precision=lax.Precision.HIGHEST, preferred_element_type=jnp.float32
    ).astype(jnp.int32)

    def first_part(weight_first, gain_first, shift_first):
        return first_layer(owned_wave, weight_first, gain_first, shift_first)

    activated, first_pull = jax.vjp(first_part, first_weight, first_gain, first_shift)
    rounded = activated.astype(jnp.bfloat16)
    patches = make_patches(rounded, row_total)
    whole_weight = gathered_copies(second_weight, "fsdp", 0)
    second_pre = jnp.dot(patches, whole_weight, preferred_element_type=jnp.float32)
    frame_mask = frame_mask_of(owned_length, later)

    def head_part(pre_norm, gain_second, shift_second):
        return head_loss(pre_norm, gain_second, shift_second, targets.reshape(-1), frame_mask)

    loss_sum, head_pull, raw_logvar = jax.vjp(
        head_part, second_pre, second_gain, second_shift, has_aux=True
    )
    grad_pre, grad_gain_two, grad_shift_two = head_pull(jnp.ones_like(loss_sum))
    grad_pre = grad_pre.astype(jnp.bfloat16)
    fsdp_count = lax.axis_size("fsdp")
    block_rows = second_weight.shape[0]
    piece_rows = -(-block_rows // peer_count)
    frame_rows = patches.shape[0]
    arranged = patches.reshape(frame_rows, fsdp_count, block_rows)
    arranged = arranged.reshape(frame_rows, fsdp_count, peer_count, piece_rows)
    arranged = jnp.transpose(arranged, (0, 2, 1, 3)).reshape(
        frame_rows, peer_count * fsdp_count * piece_rows
    )
    summed_piece = summed_rows(
        lax.dot_general(
            arranged, grad_pre, (((0,), (0,)), ((), ())), preferred_element_type=jnp.float32
        ),
        DP_FSDP,
        (2, 0, 1, 3),
        0,
    )
    gathered = gathered_copies(summed_piece, DP, 0)
    grad_weight_two = gathered[:block_rows]
    grad_patches = lax.dot_general(
        grad_pre, whole_weight, (((1,), (1,)), ((), ())), preferred_element_type=jnp.float32
    )
    grad_act = patch_grad(grad_patches, row_total, frames)
    grad_weight_one, grad_gain_one, grad_shift_one = first_pull(grad_act)
    summed = (
        one_axis_at_a_time(grad_weight_one, DP_FSDP),
        one_axis_at_a_time(grad_gain_one, DP_FSDP),
        one_axis_at_a_time(grad_shift_one, DP_FSDP),
        one_axis_at_a_time(grad_gain_two, DP_FSDP),
        one_axis_at_a_time(grad_shift_two, DP_FSDP),
        one_axis_at_a_time(loss_sum, DP_FSDP),
        one_axis_at_a_time(jnp.sum(frame_mask), DP_FSDP),
    )
    logvar = (raw_logvar * frame_mask).reshape(row_total, later)
    loss = summed[5] / summed[6]
    return (logvar, loss, grad_weight_two, summed[0], summed[1], summed[2], summed[3], summed[4])


def solution(mesh):
    torus = Mesh(
        mesh.devices.reshape(8, 4, 2, mesh.shape["fsdp"]), ("dp_0", "dp_1", "dp_2", "fsdp")
    )
    return jax.shard_map(
        per_device,
        mesh=torus,
        in_specs=(
            P(DP_FSDP, None),
            P(DP_FSDP),
            P(DP_FSDP),
            P(DP_FSDP, None),
            P(),
            P(),
            P(),
            P("fsdp", None),
            P(),
            P(),
        ),
        out_specs=(P(DP_FSDP, None), P(), P("fsdp", None), P(), P(), P(), P(), P()),
        check_vma=False,
    )
```

profile of v0, /device:TPU:1, one launch (start us, length us, event | category | flops | bytes accessed | tf_op | source)
XLA Modules:
  0.0 271.8 jit_solution(420147839574337199)
XLA Ops:
  11.6 14.8 %all-to-all-start = ((f32[64,1,401]{2,1,0:T(1,128)}), f32[64,1,401]{2,1,0:T(1,128)S(1)}, u32[]{:S(2)}, u32[]{:S(2)}) async-start(f32[64,1,401]{2,1,0:T(1,128)} %copy.54), calls=%async_computation | async-start | bytes 262144 | tf_op jit(solution)/shard_map/all_to_all | solution.py:22
  27.2 10.3 %all-to-all-done = f32[64,1,401]{2,1,0:T(1,128)S(1)} async-done(((f32[64,1,401]{2,1,0:T(1,128)}), f32[64,1,401]{2,1,0:T(1,128)S(1)}, u32[]{:S(2)}, u32[]{:S(2)}) %all-to-all-start) | async-done | bytes 102688 | tf_op jit(solution)/shard_map/all_to_all | solution.py:22
  37.6 2.2 broadcast_in_dim.21
  39.8 6.8 %all-to-all-start.1 = ((bf16[8,192,512]{2,1,0:T(8,128)(2,1)}), bf16[8,192,512]{2,1,0:T(8,128)(2,1)}, u32[]{:S(2)}, u32[]{:S(2)}) async-start(bf16[8,192,512]{2,1,0:T(8,128)(2,1)} %broadcast_in_dim.21), calls=%async_computation.1 | async-start | bytes 3145728 | tf_op jit(solution)/shard_map/all_to_all | solution.py:37
  50.4 4.6 %multiply_convert_fusion = (bf16[632,512]{1,0:T(8,128)(2,1)S(1)}, f32[632,512]{1,0:T(8,128)}) fusion(f32[632,512]{1,0:T(8,128)S(1)} %get-tuple-element.69, f32[512]{0:T(512)S(1)} %copy-done.5, f32[512]{0:T(512)S(1)} %copy-done.1, f32[632]{0:T(1024)S(1)} %fusion.29, f32[632]{0:T(1024)S(1)} %broadcast_multiply_fusion), kind=kLoop, calls=%fused_computation.10 | loop fusion | flops 22327296 | bytes 3244992 | tf_op jit(solution)/shard_map/convert_element_type | solution.py:201
  58.3 3.5 %copy.60 = bf16[8,39,1536]{1,0,2:T(8,128)(2,1)} copy(bf16[8,39,1536]{2,1,0:T(8,128)(2,1)S(1)} %pad_maximum_fusion.1) | data formatting | bytes 1916928 | tf_op jit(solution)/shard_map/concatenate | solution.py:99
  62.1 6.3 %reshape_reshape_reshape.3 = bf16[312,8,64,3]{0,3,2,1:T(4,128)(2,1)S(1)} reshape(bf16[8,39,1536]{1,0,2:T(8,128)(2,1)} %copy.60) | data formatting | bytes 1916928 | tf_op jit(solution)/shard_map/reshape;reshape;reshape | solution.py:220
  68.4 1.7 copy.61
  70.1 3.9 %reshape.202 = bf16[312,1536]{0,1:T(8,128)(2,1)} reshape(bf16[312,64,8,3]{0,3,2,1:T(4,128)(2,1)} %copy.61) | data formatting | bytes 1916928 | tf_op jit(solution)/shard_map/reshape | solution.py:221
  74.0 2.4 dot_general.48
  76.4 8.6 %all-to-all-done.1 = bf16[8,192,512]{2,1,0:T(8,128)(2,1)} async-done(((bf16[8,192,512]{2,1,0:T(8,128)(2,1)}), bf16[8,192,512]{2,1,0:T(8,128)(2,1)}, u32[]{:S(2)}, u32[]{:S(2)}) %all-to-all-start.1) | async-done | bytes 1572896 | tf_op jit(solution)/shard_map/all_to_all | solution.py:37
  85.0 2.5 fusion.57
  87.8 1.7 fusion.50
  92.2 2.0 copy.63
  94.2 11.8 %reduce-scatter.5.cloned.1.call-done = f32[256,3,512]{2,0,1:T(8,128)} async-done(((f32[512,3,512]{2,0,1:T(8,128)}), f32[256,3,512]{2,0,1:T(8,128)}) %reduce-scatter.5.cloned.1.call-update) | async-done | bytes 1572880 | tf_op jit(solution)/shard_map/reduce_scatter | solution.py:50
  107.8 2.1 fusion.19
  113.3 2.8 %multiply_reduce_fusion = (f32[512]{0:T(512)S(1)}, f32[632]{0:T(1024)S(1)}, f32[512]{0:T(512)S(1)}, f32[632,512]{1,0:T(8,128)S(1)}) fusion(f32[632,512]{1,0:T(8,128)S(1)} %get-tuple-element.69, f32[632]{0:T(1024)S(1)} %fusion.29, f32[632]{0:T(1024)S(1)} %broadcast_multiply_fusion, f32[512]{0:T(512)S(1)} %copy-done.1, f32[632,512]{1,0:T(8,128)} %reshape.207, ...), kind=kLoop, calls=%fused_computation.5 | loop fusion | flops 7440776 | bytes 5193120 | tf_op jit(solution)/shard_map/transpose(jvp())/reduce_sum | solution.py:73
  118.0 31.3 %reduce-scatter.7.cloned.1.call-done = f32[32,3,512]{2,0,1:T(8,128)} async-done(((f32[256,3,512]{2,0,1:T(8,128)}), f32[32,3,512]{2,0,1:T(8,128)}) %reduce-scatter.7.cloned.1.call-update) | async-done | bytes 196624 | tf_op jit(solution)/shard_map/reduce_scatter | solution.py:50
  150.2 23.4 %all-reduce.6 = (f32[]{:T(128)}, f32[]{:T(128)}, f32[10,512]{1,0:T(8,128)S(1)}, f32[512]{0:T(512)S(1)}, f32[512]{0:T(512)S(1)}, /*index=5*/f32[512]{0:T(512)S(1)}, f32[512]{0:T(512)S(1)}) all-reduce(f32[]{:T(128)} %get-tuple-element.15, f32[]{:T(128)} %get-tuple-element.14, ...), channel_id=1, replica_groups=mesh['dp_0'=8,'dp_1'=4,'dp_2'=2,'fsdp'=8] {'dp_0'}, use_global_device_ids=true, to_apply=%region_9.10 | all-reduce | flops 7170 | bytes 57360 | tf_op jit(solution)/shard_map/psum | solution.py:66
  173.6 14.8 %all-reduce.7 = (f32[]{:T(128)}, f32[]{:T(128)}, f32[10,512]{1,0:T(8,128)S(1)}, f32[512]{0:T(512)S(1)}, f32[512]{0:T(512)S(1)}, /*index=5*/f32[512]{0:T(512)S(1)}, f32[512]{0:T(512)S(1)}) all-reduce(f32[]{:T(128)} %get-tuple-element.24, f32[]{:T(128)} %get-tuple-element.25, ...), channel_id=1, replica_groups=mesh['dp_0'=8,'dp_1'=4,'dp_2'=2,'fsdp'=8] {'dp_1'}, use_global_device_ids=true, to_apply=%region_10.11 | all-reduce | flops 7170 | bytes 57360 | tf_op jit(solution)/shard_map/psum | solution.py:66
  188.3 18.9 %all-reduce.8 = (f32[]{:T(128)}, f32[]{:T(128)}, f32[10,512]{1,0:T(8,128)S(1)}, f32[512]{0:T(512)S(1)}, f32[512]{0:T(512)S(1)}, /*index=5*/f32[512]{0:T(512)S(1)}, f32[512]{0:T(512)S(1)}) all-reduce(f32[]{:T(128)} %get-tuple-element.31, f32[]{:T(128)} %get-tuple-element.32, ...), channel_id=1, replica_groups=mesh['dp_0'=8,'dp_1'=4,'dp_2'=2,'fsdp'=8] {'dp_2'}, use_global_device_ids=true, to_apply=%region_11.12 | all-reduce | flops 7170 | bytes 57360 | tf_op jit(solution)/shard_map/psum | solution.py:66
  207.2 24.6 %all-reduce.10 = (f32[]{:T(128)}, f32[]{:T(128)}, f32[8,3,512]{2,0,1:T(8,128)S(1)}, f32[10,512]{1,0:T(8,128)}, f32[512]{0:T(512)}, /*index=5*/f32[512]{0:T(512)}, f32[512]{0:T(512)}, f32[512]{0:T(512)}) all-reduce(f32[]{:T(128)} %get-tuple-element.38, ...), channel_id=1, replica_groups=mesh['dp_0'=8,'dp_1'=4,'dp_2'=2,'fsdp'=8] {'fsdp'}, use_global_device_ids=true, to_apply=%region_12.13 | all-reduce | flops 19458 | bytes 155664 | tf_op jit(solution)/shard_map/psum | solution.py:66
  233.3 12.2 %all-to-all-start.2 = ((f32[64,3,512]{2,1,0:T(4,128)}), f32[64,3,512]{2,1,0:T(4,128)S(1)}, u32[]{:S(2)}, u32[]{:S(2)}) async-start(f32[64,3,512]{2,1,0:T(4,128)} %broadcast_in_dim.26), calls=%async_computation.5 | async-start | bytes 1048576 | tf_op jit(solution)/shard_map/all_to_all | solution.py:37
  246.8 16.4 %all-to-all-done.2 = f32[64,3,512]{2,1,0:T(4,128)S(1)} async-done(((f32[64,3,512]{2,1,0:T(4,128)}), f32[64,3,512]{2,1,0:T(4,128)S(1)}, u32[]{:S(2)}, u32[]{:S(2)}) %all-to-all-start.2) | async-done | bytes 393248 | tf_op jit(solution)/shard_map/all_to_all | solution.py:37
  (87 shorter events, 25.7 us)
Async XLA Ops:
  7.2 41.5 %copy-start = (f32[10,512]{1,0:T(8,128)S(1)}, f32[10,512]{1,0:T(8,128)}, u32[]{:S(2)}) copy-start(f32[10,512]{1,0:T(8,128)} %param.14) | copy-start | bytes 61444
  11.6 26.0 %all-to-all-start = ((f32[64,1,401]{2,1,0:T(1,128)}), f32[64,1,401]{2,1,0:T(1,128)S(1)}, u32[]{:S(2)}, u32[]{:S(2)}) async-start(f32[64,1,401]{2,1,0:T(1,128)} %copy.54), calls=%async_computation | async-start | bytes 262144 | tf_op jit(solution)/shard_map/all_to_all | solution.py:22
  39.8 45.2 %all-to-all-start.1 = ((bf16[8,192,512]{2,1,0:T(8,128)(2,1)}), bf16[8,192,512]{2,1,0:T(8,128)(2,1)}, u32[]{:S(2)}, u32[]{:S(2)}) async-start(bf16[8,192,512]{2,1,0:T(8,128)(2,1)} %broadcast_in_dim.21), calls=%async_computation.1 | async-start | bytes 3145728 | tf_op jit(solution)/shard_map/all_to_all | solution.py:37
  46.6 59.4 %reduce-scatter.5.cloned.1.call-start = ((), (), s32[]{:S(2)}) async-start(), calls=%async_computation.6 | async-start | bytes 4718592 | tf_op jit(solution)/shard_map/reduce_scatter | solution.py:50
  48.7 1.6 copy-start.1
  48.7 1.6 copy-start.5
  85.0 2.7 %copy-start.2 = (f32[512]{0:T(512)S(1)}, f32[512]{0:T(512)}, u32[]{:S(2)}) copy-start(f32[512]{0:T(512)} %param.18) | copy-start | bytes 6148
  85.0 2.8 %copy-start.4 = (f32[512]{0:T(512)S(1)}, f32[512]{0:T(512)}, u32[]{:S(2)}) copy-start(f32[512]{0:T(512)} %param.19) | copy-start | bytes 6148
  94.2 55.1 %reduce-scatter.7.cloned.1.call-start = ((), (), s32[]{:S(2)}) async-start(), calls=%async_computation.7 | async-start | bytes 1769472 | tf_op jit(solution)/shard_map/reduce_scatter | solution.py:50
  106.0 101.2 %reduce-scatter.9.cloned.1.call-start = ((), (), s32[]{:S(2)}) async-start(), calls=%async_computation.8 | async-start | bytes 245760 | tf_op jit(solution)/shard_map/reduce_scatter | solution.py:50
  113.3 2.9 %copy-start.3 = (f32[8,39]{1,0:T(8,128)S(1)}, f32[8,39]{1,0:T(8,128)}, u32[]{:S(2)}) copy-start(f32[8,39]{1,0:T(8,128)} %param.13) | copy-start | bytes 3748
  233.3 29.9 %all-to-all-start.2 = ((f32[64,3,512]{2,1,0:T(4,128)}), f32[64,3,512]{2,1,0:T(4,128)S(1)}, u32[]{:S(2)}, u32[]{:S(2)}) async-start(f32[64,3,512]{2,1,0:T(4,128)} %broadcast_in_dim.26), calls=%async_computation.5 | async-start | bytes 1048576 | tf_op jit(solution)/shard_map/all_to_all | solution.py:37
Sparse Core Ops, SparseCore 0:
  94.3 11.6 reduce-scatter.4
  109.1 40.1 reduce-scatter.6
  152.3 25.7 reduce-scatter.8
where the time goes:
time: 273 us; the launch traced here: 272 us
  blocking collectives  81.6 us (30%)
  waiting for transfers between devices  78.4 us (29%)
  local copies, waits for them, and re-layouts  35.2 us (13%)
  starting transfers between devices  34.2 us (13%)
  between operations  16.6 us (6%)
  other arithmetic  15.6 us (6%)
  matrix products  10.1 us (4%)
    psum x4, blocking collectives, one_axis_at_a_time(): return functools.reduce(lax.psum, axes, array)  81.6 us
    reduce_scatter x3, waiting for transfers between devices, own_block(): pieces = lax.psum_scatter(pieces, axes[k], scatter_dimension=0, tiled=True)  43 us
    all_to_all x2, waiting for transfers between devices, copy_for_each(): return lax.all_to_all(copies, axis, split_axis=0, concat_axis=0, tiled=True)  25 us
    all_to_all x2, starting transfers between devices, copy_for_each(): return lax.all_to_all(copies, axis, split_axis=0, concat_axis=0, tiled=True)  19 us
    all_to_all x1, starting transfers between devices, side_by_side(): lax.all_to_all(both, axis, split_axis=split_dim, concat_axis=concat_dim,...  14.8 us
    all_to_all x1, waiting for transfers between devices, side_by_side(): lax.all_to_all(both, axis, split_axis=split_dim, concat_axis=concat_dim,...  10.3 us
    another operation x1, local copies, waits for them, and re-layouts, per_device(): arranged = arranged.reshape(frame_rows, fsdp_count, peer_count, piece_rows)  6.3 us
  transfers between devices with their start and end apart: 6, of which 5 were waited for; matrix products, arithmetic and copies ran while one was open for 16% of the time, Pallas kernels for 0%

commit v1 on v0

v1 whole, which is shorter than its diff:
```python
import functools

import jax
import jax.numpy as jnp
from jax import lax
from jax.experimental import pallas as pl
from jax.experimental.pallas import tpu as pltpu
from jax.sharding import Mesh
from jax.sharding import PartitionSpec as P

DP = ("dp_0", "dp_1", "dp_2")
DP_FSDP = ("dp_0", "dp_1", "dp_2", "fsdp")
AXES = {"z": "dp_0", "x": "dp_1", "c": "dp_2", "y": "fsdp"}
EPS = 1e-05
C = 512
F32 = jnp.float32
BF16 = jnp.bfloat16
MESH = pl.DeviceIdType.MESH
TN = (((0,), (0,)), ((), ()))
NT = (((1,), (1,)), ((), ()))
TILES = 16
CHUNK = 32


class Exchange:
    def __init__(self, axis, size, me, src, dst, sems):
        self.axis, self.size, self.me = axis, size, me
        self.src, self.dst = src, dst
        self.send_sems, self.recv_sems = sems

    def _copy(self, r, slot, peer):
        return pltpu.make_async_remote_copy(
            src_ref=self.src(peer),
            dst_ref=self.dst(slot),
            send_sem=self.send_sems.at[r],
            recv_sem=self.recv_sems.at[r],
            device_id={AXES[self.axis]: peer},
            device_id_type=MESH,
        )

    def start(self):
        for r in range(1, self.size):
            self._copy(r, self.me, lax.rem(self.me + r, self.size)).start()

    def sender(self, r):
        return lax.rem(self.me + self.size - r, self.size)

    def wait_recv(self, r):
        s = self.sender(r)
        self._copy(r, s, s).wait_recv()

    def wait_all_recv(self):
        for r in range(1, self.size):
            self.wait_recv(r)

    def wait_sends(self):
        for r in range(1, self.size):
            self._copy(r, self.me, lax.rem(self.me + r, self.size)).wait_send()


def dot(a, b, dims=(((1,), (0,)), ((), ()))):
    return lax.dot_general(a, b, dims, preferred_element_type=F32)


def split2(v):
    hi = v.astype(BF16)
    return hi, (v - hi.astype(F32)).astype(BF16)


def split3(v):
    hi, mid = split2(v)
    return hi, mid, (v - hi.astype(F32) - mid.astype(F32)).astype(BF16)


def gelu_parts(u):
    a = jnp.abs(u)
    t = 1.0 / (1.0 + 0.23164190 * a)
    e = jnp.exp(u * u * -0.5)
    poly = 0.5 * 1.061405429
    poly = poly * t - 0.5 * 1.453152027
    poly = poly * t + 0.5 * 1.421413741
    poly = poly * t - 0.5 * 0.284496736
    poly = poly * t + 0.5 * 0.254829592
    tail = poly * t * e
    cdf = jnp.where(u >= 0.0, 1.0 - tail, tail)
    return u * cdf, cdf + u * (e * 0.3989422804014327)


def fold8(v):
    return v.reshape(v.shape[0] // 8, 8, v.shape[1]).sum(axis=0)


def kernel(sizes, *refs):
    Z, X, Y = sizes
    (wave_ref, blk_ref, fw_ref, g1_ref, s1_ref, w_ref, g2_ref, s2_ref,
     lv_ref, loss_ref, gw2_ref, gw1_ref, gg1_ref, gs1_ref, gg2_ref, gs2_ref,
     W, TG, LG, wpad, wconv, xcol, xh, dg, rs, act, act_peer, v, tsel, vmask, gf, G, g_peer,
     DA, DB, RA, RB, A1, B1, RA2, RB2, XR, dact, gph, gpm, S, S_peer, SY, S1, SZ, SX, SA, pick,
     w_sy, w_ry, w_sx, w_rx, w_sc, w_rc, tx_s, tx_r, tz_s, tz_r, lx_s, lx_r, lz_s, lz_r,
     a_s, a_r, b_s, b_r, a2_s, a2_r, b2_s, b2_r, x_s, x_r, z_s, z_r,
     sy_s, sy_r, sz_s, sz_r, sx_s, sx_r, sa_s, sa_r, c_s, c_r) = refs
    z, x, c, y = (lax.axis_index(AXES[k]) for k in "zxcy")
    other = 1 - c
    RY = W.shape[1]
    RX = RY // X
    RZ = RY // Z
    rows = 8 * 40
    per_y = TILES // Y
    dp = Z * X * 2
    readers = dp * 8
    me_dp = (z * X + x) * 2 + c

    barrier = pltpu.get_barrier_semaphore()
    for axis, size, me in (("c", 2, c), ("x", X, x), ("y", Y, y), ("z", Z, z)):
        for r in range(1, size):
            pl.semaphore_signal(
                barrier, inc=1, device_id={AXES[axis]: lax.rem(me + r, size)}, device_id_type=MESH
            )

    def core_copy(k, src, dst):
        return pltpu.make_async_remote_copy(
            src_ref=src, dst_ref=dst, send_sem=c_s.at[k], recv_sem=c_r.at[k],
            device_id={AXES["c"]: other}, device_id_type=MESH,
        )

    half = pl.ds(pl.multiple_of(c * 256, 256), 256)
    other_half = pl.ds(pl.multiple_of(other * 256, 256), 256)

    W[y] = w_ref[...]
    TG[z, x, c] = blk_ref[...]
    quarter = pl.ds(pl.multiple_of(x * RX, RX), RX)

    def quarter_of(k):
        return pl.ds(pl.multiple_of(k * RX, RX), RX)

    pl.semaphore_wait(barrier, 1 + (X - 1) + (Y - 1) + (Z - 1))

    wy = Exchange("y", Y, y, lambda p: W.at[y, quarter, half], lambda s: W.at[s, quarter, half], (w_sy, w_ry))
    wy.start()

    def wx(k, slot):
        return Exchange(
            "x", X, x, lambda p: W.at[slot, quarter, half],
            lambda s: W.at[slot, quarter_of(s), half], (w_sx.at[k], w_rx.at[k]),
        )

    def wc_send(k, slot):
        return pltpu.make_async_remote_copy(
            src_ref=W.at[slot, :, half], dst_ref=W.at[slot, :, half], send_sem=w_sc.at[k],
            recv_sem=w_rc.at[k], device_id={AXES["c"]: other}, device_id_type=MESH,
        )

    def wc_recv(k, slot):
        return pltpu.make_async_remote_copy(
            src_ref=W.at[slot, :, other_half], dst_ref=W.at[slot, :, other_half], send_sem=w_sc.at[k],
            recv_sem=w_rc.at[k], device_id={AXES["c"]: other}, device_id_type=MESH,
        )

    tc_send = core_copy(0, TG.at[z, x, c], TG.at[z, x, c])
    tc_recv = core_copy(0, TG.at[z, x, other], TG.at[z, x, other])
    tc_send.start()
    tx = Exchange("x", X, x, lambda p: TG.at[z, x], lambda s: TG.at[z, s], (tx_s, tx_r))
    tz = Exchange("z", Z, z, lambda p: TG.at[z], lambda s: TG.at[s], (tz_s, tz_r))

    wpad[...] = jnp.zeros_like(wpad)
    wpad[:, : wave_ref.shape[1]] = wave_ref[...]
    samples = lax.broadcasted_iota(jnp.int32, (512, 128), 0).astype(F32)
    lanes = lax.broadcasted_iota(jnp.int32, (512, 128), 1).astype(F32)
    tap = samples - 5.0 * jnp.floor((samples + 0.5) * 0.2)
    place_hi = jnp.where((lanes == tap) | (lanes == tap + 16.0), 1.0, 0.0).astype(BF16)
    place_mid = jnp.where(lanes == tap + 8.0, 1.0, 0.0).astype(BF16)
    frame = lax.broadcasted_iota(jnp.int32, (40, 512), 0)
    offset = lax.broadcasted_iota(jnp.int32, (40, 512), 1) - 10 * frame
    in_even = (offset >= 0) & (offset < 5)
    in_odd = (offset >= 5) & (offset < 10)
    even, odd = [], []
    for k in range(8):
        row = jnp.broadcast_to(wpad[k : k + 1, :], (40, 512))
        even.append(jnp.where(in_even, row, 0.0))
        odd.append(jnp.where(in_odd, row, 0.0))
    blocks = []
    for parts in (even, odd):
        hi, mid = split2(jnp.concatenate(parts, axis=0))
        blocks.append(dot(hi, place_hi) + dot(mid, place_mid))
    even_block, odd_block = blocks
    xcol[:rows] = (even_block + pltpu.roll(odd_block, 32, 1)).astype(BF16)
    xcol[rows:] = (odd_block + pltpu.roll(pltpu.roll(even_block, rows - 1, 0), 32, 1)).astype(BF16)
    wconv[...] = jnp.zeros_like(wconv)
    fw = fw_ref[...]
    fw_hi = fw.astype(BF16).astype(F32)
    fw_mid = (fw - fw_hi).astype(BF16).astype(F32)
    for base, taps in ((0, slice(0, 5)), (32, slice(5, 10))):
        wconv[base : base + 5] = fw_hi[taps]
        wconv[base + 8 : base + 13] = fw_hi[taps]
        wconv[base + 16 : base + 21] = fw_mid[taps]
    xh[...] = dot(xcol[...], wconv[...].astype(BF16))

    g1, s1 = g1_ref[...], s1_ref[...]

    def forward_chunk(i, carry):
        at = pl.ds(pl.multiple_of(i * CHUNK, CHUNK), CHUNK)
        pre = xh[at, :]
        centered = pre - jnp.mean(pre, axis=1, keepdims=True)
        inv = lax.rsqrt(jnp.mean(centered * centered, axis=1, keepdims=True) + EPS)
        normed = centered * inv
        value, slope = gelu_parts(normed * g1 + s1)
        xh[at, :] = normed
        dg[at, :] = slope
        rs[at, :] = jnp.broadcast_to(inv, (CHUNK, 128))
        act[at, :] = value.astype(BF16)
        return carry

    chunks = 2 * rows // CHUNK
    lax.fori_loop(0, chunks // 2, forward_chunk, 0)
    tc_recv.wait_recv()
    tx.start()
    for r in range(1, Y):
        wy.wait_recv(r)
        wx(r, wy.sender(r)).start()
    lax.fori_loop(chunks // 2, chunks, forward_chunk, 0)
    act_send = core_copy(1, act, act_peer)
    act_send.start()
    tx.wait_all_recv()
    tz.start()
    for r in range(1, Y):
        slot = wy.sender(r)
        wx(r, slot).wait_all_recv()
        wc_send(r, slot).start()

    tz.wait_all_recv()
    table = TG[...].reshape(readers, 128)
    owner_col = table[:, 39:40]
    r8 = lax.broadcasted_iota(jnp.int32, (8, 128), 0)
    l8 = lax.broadcasted_iota(jnp.int32, (8, 128), 1)
    mine = blk_ref[...]
    owner_row = jnp.sum(jnp.where(r8 == l8, mine[:, 39:40], 0.0), axis=0, keepdims=True)
    rr = lax.broadcasted_iota(jnp.int32, (readers, 128), 0)
    ll = lax.broadcasted_iota(jnp.int32, (readers, 128), 1)
    before = jnp.sum(
        jnp.where((owner_col == owner_row) & (rr < me_dp * 8), 1.0, 0.0), axis=0, keepdims=True
    )
    wanted = owner_row * 8.0 + before
    one_hot = jnp.where((rr.astype(F32) == wanted) & (ll < 8), 1.0, 0.0).astype(BF16)
    found = sum(dot(one_hot, part, TN) for part in split3(table))
    tsel[...] = found[:8]
    vmask[...] = jnp.where(l8.astype(F32) < mine[:, 40:41], 1.0, 0.0)
    flags = jnp.where(owner_col == me_dp.astype(F32), 1.0, 0.0)
    flags = jnp.broadcast_to(flags, (readers, 128))
    lower = lax.broadcasted_iota(jnp.int32, (readers, readers), 0) > lax.broadcasted_iota(
        jnp.int32, (readers, readers), 1
    )
    place = dot(jnp.where(lower, 1.0, 0.0).astype(BF16), flags.astype(BF16))
    pick[...] = jnp.where((flags > 0.5) & (place == ll.astype(F32)), 1.0, 0.0).astype(BF16)

    for r in range(1, Y):
        slot = wy.sender(r)
        wc_recv(r, slot).wait_recv()

    def tap_weight(q):
        return W[...].reshape(3 * C, C)[q * C : (q + 1) * C]

    act_even, act_odd = act[:rows], act[rows:]
    later = dot(act_even, tap_weight(2))
    v[...] = dot(act_even, tap_weight(0)) + dot(act_odd, tap_weight(1)) + pltpu.roll(later, rows - 1, 0)

    g2, s2 = g2_ref[...], s2_ref[...]
    eye = lax.broadcasted_iota(jnp.int32, (40, 128), 0) == lax.broadcasted_iota(jnp.int32, (40, 128), 1)

    def head_row(k, carry):
        gain_sum, shift_sum, misfit_sum, count = carry
        at = pl.ds(pl.multiple_of(k * 40, 8), 40)
        target = jnp.sum(jnp.where(eye, tsel[pl.ds(k, 1), :], 0.0), axis=1, keepdims=True)
        mask = jnp.sum(jnp.where(eye, vmask[pl.ds(k, 1), :], 0.0), axis=1, keepdims=True)
        pre = v[at, :]
        centered = pre - jnp.mean(pre, axis=1, keepdims=True)
        inv = lax.rsqrt(jnp.mean(centered * centered, axis=1, keepdims=True) + EPS)
        normed = centered * inv
        value, slope = gelu_parts(normed * g2 + s2)
        centered = value - jnp.mean(value, axis=1, keepdims=True)
        spread = jnp.mean(centered * centered, axis=1, keepdims=True) + EPS
        raw = jnp.log(spread)
        misfit = raw - target
        LG[z, x, c, pl.ds(k, 1), :] = jnp.sum(jnp.where(eye, raw * mask, 0.0), axis=0, keepdims=True)
        du = centered * (mask * misfit * (4.0 / C) / spread) * slope
        dx = du * g2
        m1 = jnp.mean(dx, axis=1, keepdims=True)
        m2 = jnp.mean(dx * normed, axis=1, keepdims=True)
        gf[at, :] = inv * (dx - m1 - normed * m2)
        return (
            gain_sum + fold8(du * normed),
            shift_sum + fold8(du),
            misfit_sum + mask * misfit * misfit,
            count + mask,
        )

    zero = jnp.zeros((8, C), F32)
    column = jnp.zeros((40, 1), F32)
    gain_sum2, shift_sum2, misfit_sum, count = lax.fori_loop(0, 8, head_row, (zero, zero, column, column))
    lc_send = core_copy(3, LG.at[z, x, c], LG.at[z, x, c])
    lc_recv = core_copy(3, LG.at[z, x, other], LG.at[z, x, other])
    lc_send.start()
    grad = gf[...]
    grad_late = pltpu.roll(grad, 1, 0)
    for h in range(2):
        G[h, 0] = grad[:, 256 * h : 256 * (h + 1)].astype(BF16)
        G[h, 1] = grad_late[:, 256 * h : 256 * (h + 1)].astype(BF16)
    g_send = core_copy(2, G.at[other], g_peer)
    g_send.start()

    def column_grads(acts, grads):
        e, o = acts[:rows], acts[rows:]
        return dot(e, grads[0], TN), dot(o, grads[0], TN), dot(e, grads[1], TN)

    own = column_grads(act, G.at[c])
    lx = Exchange("x", X, x, lambda p: LG.at[z, x], lambda s: LG.at[z, s], (lx_s, lx_r))
    lz = Exchange("z", Z, z, lambda p: LG.at[z], lambda s: LG.at[s], (lz_s, lz_r))
    act_send.wait_recv()
    g_send.wait_recv()
    peers = column_grads(act_peer, g_peer)
    total = jnp.concatenate([a + b for a, b in zip(own, peers)], axis=0)
    DA[...] = total[:, :128].reshape(Y, RY, 128)
    DB[...] = total[:, 128:].reshape(Y, Z, RZ, 128)
    ya = Exchange("y", Y, y, lambda p: DA.at[p], lambda s: RA.at[s], (a_s, a_r))
    zb = Exchange("z", Z, z, lambda p: DB.at[:, p], lambda s: RB.at[s], (b_s, b_r))
    ya.start()
    zb.start()
    lc_recv.wait_recv()
    lx.start()

    def whole_grad(k):
        return jnp.concatenate([G[0, k], G[1, k]], axis=1)

    now, late = whole_grad(0), whole_grad(1)
    dact[:rows] = dot(now, tap_weight(0), NT) + dot(late, tap_weight(2), NT)
    dact[rows:] = dot(now, tap_weight(1), NT)

    def backward_chunk(i, carry):
        gain_sum, shift_sum = carry
        at = pl.ds(pl.multiple_of(i * CHUNK, CHUNK), CHUNK)
        normed = xh[at, :]
        du = dact[at, :] * dg[at, :]
        dx = du * g1
        m1 = jnp.mean(dx, axis=1, keepdims=True)
        m2 = jnp.mean(dx * normed, axis=1, keepdims=True)
        dpre = rs[at, :1] * (dx - m1 - normed * m2)
        hi, mid = split2(dpre)
        gph[at, :] = hi
        gpm[at, :] = mid
        return gain_sum + fold8(du * normed), shift_sum + fold8(du)

    gain_sum1, shift_sum1 = lax.fori_loop(0, chunks, backward_chunk, (zero, zero))
    taps = dot(xcol[...], gph[...], TN) + dot(xcol[...], gpm[...], TN)
    ri = lax.broadcasted_iota(jnp.int32, (8, C), 0)
    li = lax.broadcasted_iota(jnp.int32, (8, C), 1)

    def line(vector, k):
        return jnp.where(ri == k, jnp.sum(vector, axis=0, keepdims=True), 0.0)

    loss_line = jnp.where(
        li == 0,
        jnp.sum(misfit_sum, axis=0, keepdims=True),
        jnp.where(li == 1, jnp.sum(count, axis=0, keepdims=True), 0.0),
    )
    groups = [
        taps[0:8] + taps[8:16],
        taps[32:40] + taps[40:48],
        line(gain_sum1, 0) + line(shift_sum1, 1) + line(gain_sum2, 2) + line(shift_sum2, 3)
        + jnp.where(ri == 4, loss_line, 0.0),
        zero,
    ]
    for i, group in enumerate(groups):
        for j in range(4):
            S[4 * i + j] = group[:, 128 * j : 128 * (j + 1)]
    sc = core_copy(4, S, S_peer)
    sc.start()
    lx.wait_all_recv()
    lz.start()
    sc.wait_recv()
    S1[...] = (S[...] + S_peer[...]).reshape(Y, per_y, 8, 128)
    sy = Exchange("y", Y, y, lambda p: S1.at[p], lambda s: SY.at[s], (sy_s, sy_r))
    sy.start()

    total = DA[y]
    for r in range(1, Y):
        ya.wait_recv(r)
        total = total + RA[ya.sender(r)]
    A1[...] = total.reshape(Z, RZ, 128)
    za = Exchange("z", Z, z, lambda p: A1.at[p], lambda s: RA2.at[s], (a2_s, a2_r))
    za.start()
    total = DB[:, z]
    for r in range(1, Z):
        zb.wait_recv(r)
        total = total + RB[zb.sender(r)]
    B1[...] = total
    yb = Exchange("y", Y, y, lambda p: B1.at[p], lambda s: RB2.at[s], (b2_s, b2_r))
    yb.start()
    sy.wait_all_recv()
    SY[y] = S1[y]
    total = SY[0]
    for k in range(1, Y):
        total = total + SY[k]
    SZ[z] = total
    sz = Exchange("z", Z, z, lambda p: SZ.at[z], lambda s: SZ.at[s], (sz_s, sz_r))
    sz.start()

    first = A1[z]
    for r in range(1, Z):
        za.wait_recv(r)
        first = first + RA2[za.sender(r)]
    second = B1[y]
    for r in range(1, Y):
        yb.wait_recv(r)
        second = second + RB2[yb.sender(r)]
    XR[x] = jnp.concatenate([first, second], axis=1)
    xs = Exchange("x", X, x, lambda p: XR.at[x], lambda s: XR.at[s], (x_s, x_r))
    xs.start()
    sz.wait_all_recv()
    total = SZ[0]
    for k in range(1, Z):
        total = total + SZ[k]
    SX[x] = total
    sx = Exchange("x", X, x, lambda p: SX.at[x], lambda s: SX.at[s], (sx_s, sx_r))
    sx.start()

    def rows_of(k):
        return pl.ds(pl.multiple_of(k * RZ, 8), RZ)

    xs.wait_all_recv()
    total = XR[0]
    for k in range(1, X):
        total = total + XR[k]
    gw2_ref[rows_of(z), half] = total
    zg = Exchange(
        "z", Z, z, lambda p: gw2_ref.at[rows_of(z), half], lambda s: gw2_ref.at[rows_of(s), half], (z_s, z_r)
    )
    zg.start()
    sx.wait_all_recv()
    total = SX[0]
    for k in range(1, X):
        total = total + SX[k]
    SA[y] = total
    sa = Exchange("y", Y, y, lambda p: SA.at[y], lambda s: SA.at[s], (sa_s, sa_r))
    sa.start()

    lz.wait_all_recv()
    logs = LG[...].reshape(readers, 128)
    picked = sum(dot(pick[...], part, TN) for part in split3(logs))
    lv_ref[...] = picked[:8, : lv_ref.shape[1]]

    zg.wait_all_recv()
    fin_send = core_copy(5, gw2_ref.at[:, half], gw2_ref.at[:, half])
    fin_recv = core_copy(5, gw2_ref.at[:, other_half], gw2_ref.at[:, other_half])
    fin_send.start()

    sa.wait_all_recv()
    done = SA[...].reshape(TILES, 8, 128)

    def wide(i):
        return jnp.concatenate([done[4 * i + j] for j in range(4)], axis=1)

    gw1_ref[0:5] = wide(0)[0:5]
    gw1_ref[5:10] = wide(1)[0:5]
    norms = wide(2)
    gg1_ref[...] = norms[0:1]
    gs1_ref[...] = norms[1:2]
    gg2_ref[...] = norms[2:3]
    gs2_ref[...] = norms[3:4]
    loss_ref[...] = norms[4:5, 0:1] / norms[4:5, 1:2]
    fin_recv.wait_recv()

    for e in (wy, tx, tz, lx, lz, ya, zb, za, yb, xs, zg, sy, sz, sx, sa):
        e.wait_sends()
    for r in range(1, Y):
        slot = wy.sender(r)
        wx(r, slot).wait_sends()
        wc_send(r, slot).wait_send()
    for copy in (tc_send, act_send, g_send, lc_send, sc, fin_send):
        copy.wait_send()


def per_device(sizes, waveform, lengths, owner_of, targets, first_weight, first_gain, first_shift,
               second_weight, second_gain, second_shift):
    Z, X, Y = sizes
    row_total, later = targets.shape
    valid = ((lengths - 10) // 5 - 2) // 2 + 1
    block = jnp.concatenate(
        [
            targets,
            owner_of.astype(F32)[:, None],
            valid.astype(F32)[:, None],
            jnp.zeros((row_total, 128 - later - 2), F32),
        ],
        axis=1,
    )
    RY = second_weight.shape[0]
    RZ = RY // Z
    rows = 320
    dma = pltpu.SemaphoreType.DMA
    vm = pltpu.VMEM
    per_y = TILES // Y
    scratch = [
        vm((Y, RY, C), BF16), vm((Z, X, 2, 8, 128), F32), vm((Z, X, 2, 8, 128), F32),
        vm((8, 512), F32), vm((128, C), F32), vm((2 * rows, 128), BF16),
        vm((2 * rows, C), F32), vm((2 * rows, C), F32), vm((2 * rows, 128), F32),
        vm((2 * rows, C), BF16), vm((2 * rows, C), BF16), vm((rows, C), F32),
        vm((8, 128), F32), vm((8, 128), F32), vm((rows, C), F32),
        vm((2, 2, rows, 256), BF16), vm((2, rows, 256), BF16),
        vm((Y, RY, 128), F32), vm((Y, Z, RZ, 128), F32), vm((Y, RY, 128), F32), vm((Z, Y, RZ, 128), F32),
        vm((Z, RZ, 128), F32), vm((Y, RZ, 128), F32), vm((Z, RZ, 128), F32), vm((Y, RZ, 128), F32),
        vm((X, RZ, 256), F32), vm((2 * rows, C), F32), vm((2 * rows, C), BF16), vm((2 * rows, C), BF16),
        vm((TILES, 8, 128), F32), vm((TILES, 8, 128), F32), vm((Y, per_y, 8, 128), F32),
        vm((Y, per_y, 8, 128), F32), vm((Z, per_y, 8, 128), F32), vm((X, per_y, 8, 128), F32),
        vm((Y, per_y, 8, 128), F32), vm((Z * X * 2 * 8, 128), BF16),
        dma((Y,)), dma((Y,)), dma((Y, X)), dma((Y, X)), dma((Y,)), dma((Y,)),
        dma((X,)), dma((X,)), dma((Z,)), dma((Z,)), dma((X,)), dma((X,)), dma((Z,)), dma((Z,)),
        dma((Y,)), dma((Y,)), dma((Z,)), dma((Z,)), dma((Z,)), dma((Z,)), dma((Y,)), dma((Y,)),
        dma((X,)), dma((X,)), dma((Z,)), dma((Z,)),
        dma((Y,)), dma((Y,)), dma((Z,)), dma((Z,)), dma((X,)), dma((X,)), dma((Y,)), dma((Y,)),
        dma((8,)), dma((8,)),
    ]
    shapes = [
        (row_total, later), (1, 1), (RY, C), (10, C), (1, C), (1, C), (1, C), (1, C),
    ]
    whole = pl.BlockSpec(memory_space=pltpu.VMEM)
    out = pl.pallas_call(
        functools.partial(kernel, sizes),
        out_shape=[jax.ShapeDtypeStruct(s, F32) for s in shapes],
        in_specs=[whole] * 8,
        out_specs=[whole] * len(shapes),
        scratch_shapes=scratch,
        compiler_params=pltpu.CompilerParams(
            collective_id=0, has_side_effects=True, vmem_limit_bytes=56 * 2**20
        ),
    )(
        waveform, block, first_weight, first_gain[None], first_shift[None], second_weight,
        second_gain[None], second_shift[None],
    )
    lv, loss, gw2, gw1, gg1, gs1, gg2, gs2 = out
    return lv, loss[0, 0], gw2, gw1, gg1[0], gs1[0], gg2[0], gs2[0]


def solution(mesh):
    dp, fsdp = mesh.shape["dp"], mesh.shape["fsdp"]
    x = 4 if dp >= 64 else 2
    z = dp // (2 * x)
    torus = Mesh(mesh.devices.reshape(z, x, 2, fsdp), ("dp_0", "dp_1", "dp_2", "fsdp"))
    return jax.shard_map(
        functools.partial(per_device, (z, x, fsdp)),
        mesh=torus,
        in_specs=(
            P(DP_FSDP, None), P(DP_FSDP), P(DP_FSDP), P(DP_FSDP, None), P(), P(), P(),
            P("fsdp", None), P(), P(),
        ),
        out_specs=(P(DP_FSDP, None), P(), P("fsdp", None), P(), P(), P(), P(), P()),
        check_vma=False,
    )
```

time: 273 us -> 96.9 us (0.35)
  Pallas kernels: 0 us -> 85.1 us
  blocking collectives: 81.6 us -> 0 us
  waiting for transfers between devices: 78.4 us -> 0 us
  starting transfers between devices: 34.2 us -> 0 us
  local copies, waits for them, and re-layouts: 35.2 us -> 8.32 us
  other arithmetic: 15.6 us -> 0.69 us
  between operations: 16.6 us -> 2.43 us
  matrix products: 10.1 us -> 0 us
    pallas_call x0 -> x1, Pallas kernels: none -> 85.1 us  [per_device(): pl.pallas_call(functools.partial(kernel, sizes), out_shape=[jax.ShapeDtyp...]
    psum x4 -> x0, blocking collectives: 81.6 us -> none  [one_axis_at_a_time(): return functools.reduce(lax.psum, axes, array)]
    reduce_scatter x3 -> x0, waiting for transfers between devices: 43 us -> none  [own_block(): pieces = lax.psum_scatter(pieces, axes[k], scatter_dimension=0, tiled=True)]
    all_to_all x3 -> x0, waiting for transfers between devices: 35.3 us -> none  [the longest x2 25 us: copy_for_each(): return lax.all_to_all(copies, axis, split_axis=0, concat_axis=0, tiled=True)]
    all_to_all x3 -> x0, starting transfers between devices: 33.8 us -> none  [the longest x2 19 us: copy_for_each(): return lax.all_to_all(copies, axis, split_axis=0, concat_axis=0, tiled=True)]
    dot_general x9 -> x0, matrix products: 10.1 us -> none  [the longest x1 2.48 us: per_device(): jnp.dot(patches, whole_weight, preferred_element_type=jnp.float32)]
    reduce_sum x11 -> x0, other arithmetic: 9.35 us -> none  [the longest x2 3.59 us: layer_norm(): return centered * lax.rsqrt(row_var + epsilon) * norm_gain + norm_shift]
    reshape x8 -> x0, local copies, waits for them, and re-layouts: 8.67 us -> none  [the longest x1 3.94 us: per_device(): jnp.transpose(arranged, (0, 2, 1, 3))]
  transfers between devices with their start and end apart: 6 -> 0, of which waited for: 5 -> 0; matrix products, arithmetic and copies ran while one was open for 16% -> 0% of each run, Pallas kernels for 0% -> 0%
where the time goes in v1:
time: 96.9 us; the launch traced here: 96.5 us
  Pallas kernels  85.1 us (88%)
  local copies, waits for them, and re-layouts  8.32 us (9%)
  between operations  2.43 us (3%)
    pallas_call x1, Pallas kernels, per_device(): pl.pallas_call(functools.partial(kernel, sizes), out_shape=[jax.ShapeDtyp...  85.1 us
    unnamed x25, local copies, waits for them, and re-layouts  8.08 us

profile of v1, /device:TPU:1, one launch (start us, length us, event | category | flops | bytes accessed | tf_op | source)
XLA Modules:
  0.0 96.5 jit_solution(4051075196416144415)
XLA Ops:
  0.6 0.0 copy-start.7
  0.6 0.6 copy-done.7
  1.3 0.6 copy-done.8
  1.9 0.1 pad.3.clone
  2.0 0.1 copy.18
  2.1 0.1 copy.19
  2.2 0.5 copy-done.2
  2.7 0.7 maximum_maximum_fusion.refs_1_
  3.4 85.1 %shard_map.161 = (f32[8,39]{1,0:T(8,128)}, f32[1,1]{1,0:T(1,128)}, f32[192,512]{1,0:T(8,128)}, f32[10,512]{1,0:T(8,128)}, f32[1,512]{1,0:T(1,128)}, /*index=5*/f...) custom-call(f32[8,400]{1,0:T(8,128)} %refs_0_.1, f32[8,128]{1,0:T(8,128)} %maximum_maximum_fusion.refs_1_, ...), custom_call_target="tpu_custom_call" | custom-call | tf_op jit(solution)/shard_map/pallas_call | solution.py:525
  88.5 0.0 copy-start.1
  88.5 0.7 copy-done.1
  89.2 0.6 copy.28
  90.4 0.0 copy-start
  90.4 1.8 %copy.30 = f32[192,512]{1,0:T(8,128)} copy(f32[192,512]{1,0:T(8,128)} %get-tuple-element.34) | data formatting | bytes 786432
  92.2 0.0 copy-done
  92.2 0.6 copy.31
  92.8 0.1 copy-done.6
  92.8 0.6 copy.32
  93.4 0.1 copy-done.5
  93.5 0.6 copy.33
  94.1 0.1 copy-done.4
  94.2 0.6 copy.34
  94.8 0.1 copy-done.3
  94.8 0.6 copy.35
  (9 shorter events, 0.0 us)
Async XLA Ops:
  0.6 0.7 copy-start.7
  1.3 0.7 copy-start.8
  2.0 0.7 copy-start.2
  88.5 0.7 copy-start.1
  90.4 1.8 %copy-start = (f32[10,512]{1,0:T(8,128)S(1)}, f32[10,512]{1,0:T(8,128)}, u32[]{:S(2)}) copy-start(f32[10,512]{1,0:T(8,128)} %get-tuple-element.35) | copy-start | bytes 61444
  92.2 0.7 copy-start.6
  92.8 0.7 copy-start.5
  93.5 0.7 copy-start.4
  94.2 0.6 copy-start.3

commit v2 on v1

--- a/solution.py
+++ b/solution.py
@@ -20,6 +20,8 @@
 NT = (((1,), (1,)), ((), ()))
 TILES = 16
 CHUNK = 32
+LN2 = 0.6931471805599453
+LOG2E = 1.4426950408889634
 
 
 class Exchange:
@@ -92,10 +94,10 @@
 
 def kernel(sizes, *refs):
     Z, X, Y = sizes
-    (wave_ref, blk_ref, fw_ref, g1_ref, s1_ref, w_ref, g2_ref, s2_ref,
-     lv_ref, loss_ref, gw2_ref, gw1_ref, gg1_ref, gs1_ref, gg2_ref, gs2_ref,
-     W, TG, LG, wpad, wconv, xcol, xh, dg, rs, act, act_peer, v, tsel, vmask, gf, G, g_peer,
-     DA, DB, RA, RB, A1, B1, RA2, RB2, XR, dact, gph, gpm, S, S_peer, SY, S1, SZ, SX, SA, pick,
+    (wave_ref, tgt_ref, own_ref, len_ref, fw_ref, g1_ref, s1_ref, w_ref, g2_ref, s2_ref,
+     lv_ref, gw2_ref, small_ref,
+     W, TG, LG, blk, wpad, wconv, xcol, xh, dg, rs, act, act_peer, v, tsel, vmask, gf, G, g_peer,
+     DA, DB, QA, QB, RA, RB, A1, B1, RA2, RB2, XR, dact, gph, gpm, S, S_peer, SY, S1, SZ, SX, SA, pick,
      w_sy, w_ry, w_sx, w_rx, w_sc, w_rc, tx_s, tx_r, tz_s, tz_r, lx_s, lx_r, lz_s, lz_r,
      a_s, a_r, b_s, b_r, a2_s, a2_r, b2_s, b2_r, x_s, x_r, z_s, z_r,
      sy_s, sy_r, sz_s, sz_r, sx_s, sx_r, sa_s, sa_r, c_s, c_r) = refs
@@ -105,7 +107,7 @@
     RX = RY // X
     RZ = RY // Z
     rows = 8 * 40
-    per_y = TILES // Y
+    per_y = TILES // 2 // Y
     dp = Z * X * 2
     readers = dp * 8
     me_dp = (z * X + x) * 2 + c
@@ -118,16 +120,20 @@
             )
 
     def core_copy(k, src, dst):
-        return pltpu.make_async_remote_copy(
-            src_ref=src, dst_ref=dst, send_sem=c_s.at[k], recv_sem=c_r.at[k],
-            device_id={AXES["c"]: other}, device_id_type=MESH,
-        )
+        return Exchange("c", 2, c, lambda p: src, dst, (c_s.at[k], c_r.at[k]))
 
     half = pl.ds(pl.multiple_of(c * 256, 256), 256)
-    other_half = pl.ds(pl.multiple_of(other * 256, 256), 256)
 
     W[y] = w_ref[...]
-    TG[z, x, c] = blk_ref[...]
+    r8 = lax.broadcasted_iota(jnp.int32, (8, 128), 0)
+    l8 = lax.broadcasted_iota(jnp.int32, (8, 128), 1)
+    numbers = jnp.zeros((8, 128), jnp.int32)
+    for k in range(8):
+        valid = ((len_ref[k] - 10) // 5 - 2) // 2 + 1
+        numbers = jnp.where(r8 == k, jnp.where(l8 == 39, own_ref[k], valid), numbers)
+    blk[...] = numbers.astype(F32)
+    blk[:, : tgt_ref.shape[1]] = tgt_ref[...]
+    TG[z, x, c] = blk[...]
     quarter = pl.ds(pl.multiple_of(x * RX, RX), RX)
 
     def quarter_of(k):
@@ -144,23 +150,21 @@
             lambda s: W.at[slot, quarter_of(s), half], (w_sx.at[k], w_rx.at[k]),
         )
 
-    def wc_send(k, slot):
-        return pltpu.make_async_remote_copy(
-            src_ref=W.at[slot, :, half], dst_ref=W.at[slot, :, half], send_sem=w_sc.at[k],
-            recv_sem=w_rc.at[k], device_id={AXES["c"]: other}, device_id_type=MESH,
+    def half_of(k):
+        return pl.ds(pl.multiple_of(k * 256, 256), 256)
+
+    def wc(k, slot):
+        return Exchange(
+            "c", 2, c, lambda p: W.at[slot, :, half], lambda s: W.at[slot, :, half_of(s)],
+            (w_sc.at[k], w_rc.at[k]),
         )
 
-    def wc_recv(k, slot):
-        return pltpu.make_async_remote_copy(
-            src_ref=W.at[slot, :, other_half], dst_ref=W.at[slot, :, other_half], send_sem=w_sc.at[k],
-            recv_sem=w_rc.at[k], device_id={AXES["c"]: other}, device_id_type=MESH,
-        )
-
-    tc_send = core_copy(0, TG.at[z, x, c], TG.at[z, x, c])
-    tc_recv = core_copy(0, TG.at[z, x, other], TG.at[z, x, other])
-    tc_send.start()
-    tx = Exchange("x", X, x, lambda p: TG.at[z, x], lambda s: TG.at[z, s], (tx_s, tx_r))
-    tz = Exchange("z", Z, z, lambda p: TG.at[z], lambda s: TG.at[s], (tz_s, tz_r))
+    wxs = [wx(r, wy.sender(r)) for r in range(1, Y)]
+    wcs = [wc(r, wy.sender(r)) for r in range(1, Y)]
+    tz = Exchange("z", Z, z, lambda p: TG.at[z, x, c], lambda s: TG.at[s, x, c], (tz_s, tz_r))
+    tz.start()
+    tx = Exchange("x", X, x, lambda p: TG.at[:, x, c], lambda s: TG.at[:, s, c], (tx_s, tx_r))
+    tc = core_copy(0, TG.at[:, :, c], lambda s: TG.at[:, :, s])
 
     wpad[...] = jnp.zeros_like(wpad)
     wpad[:, : wave_ref.shape[1]] = wave_ref[...]
@@ -211,28 +215,25 @@
         return carry
 
     chunks = 2 * rows // CHUNK
-    lax.fori_loop(0, chunks // 2, forward_chunk, 0)
-    tc_recv.wait_recv()
+    lax.fori_loop(0, chunks // 2, forward_chunk, 0, unroll=2)
+    tz.wait_all_recv()
     tx.start()
     for r in range(1, Y):
         wy.wait_recv(r)
-        wx(r, wy.sender(r)).start()
-    lax.fori_loop(chunks // 2, chunks, forward_chunk, 0)
-    act_send = core_copy(1, act, act_peer)
+        wxs[r - 1].start()
+    lax.fori_loop(chunks // 2, chunks, forward_chunk, 0, unroll=2)
+    act_send = core_copy(1, act, lambda s: act_peer)
     act_send.start()
     tx.wait_all_recv()
-    tz.start()
+    tc.start()
     for r in range(1, Y):
-        slot = wy.sender(r)
-        wx(r, slot).wait_all_recv()
-        wc_send(r, slot).start()
-
-    tz.wait_all_recv()
+        wxs[r - 1].wait_all_recv()
+        wcs[r - 1].start()
+
+    tc.wait_all_recv()
     table = TG[...].reshape(readers, 128)
     owner_col = table[:, 39:40]
-    r8 = lax.broadcasted_iota(jnp.int32, (8, 128), 0)
-    l8 = lax.broadcasted_iota(jnp.int32, (8, 128), 1)
-    mine = blk_ref[...]
+    mine = blk[...]
     owner_row = jnp.sum(jnp.where(r8 == l8, mine[:, 39:40], 0.0), axis=0, keepdims=True)
     rr = lax.broadcasted_iota(jnp.int32, (readers, 128), 0)
     ll = lax.broadcasted_iota(jnp.int32, (readers, 128), 1)
@@ -252,9 +253,8 @@
     place = dot(jnp.where(lower, 1.0, 0.0).astype(BF16), flags.astype(BF16))
     pick[...] = jnp.where((flags > 0.5) & (place == ll.astype(F32)), 1.0, 0.0).astype(BF16)
 
-    for r in range(1, Y):
-        slot = wy.sender(r)
-        wc_recv(r, slot).wait_recv()
+    for e in wcs:
+        e.wait_all_recv()
 
     def tap_weight(q):
         return W[...].reshape(3 * C, C)[q * C : (q + 1) * C]
@@ -295,16 +295,15 @@
 
     zero = jnp.zeros((8, C), F32)
     column = jnp.zeros((40, 1), F32)
-    gain_sum2, shift_sum2, misfit_sum, count = lax.fori_loop(0, 8, head_row, (zero, zero, column, column))
-    lc_send = core_copy(3, LG.at[z, x, c], LG.at[z, x, c])
-    lc_recv = core_copy(3, LG.at[z, x, other], LG.at[z, x, other])
-    lc_send.start()
+    gain_sum2, shift_sum2, misfit_sum, count = lax.fori_loop(0, 8, head_row, (zero, zero, column, column), unroll=2)
+    lz = Exchange("z", Z, z, lambda p: LG.at[z, x, c], lambda s: LG.at[s, x, c], (lz_s, lz_r))
+    lz.start()
     grad = gf[...]
     grad_late = pltpu.roll(grad, 1, 0)
     for h in range(2):
         G[h, 0] = grad[:, 256 * h : 256 * (h + 1)].astype(BF16)
         G[h, 1] = grad_late[:, 256 * h : 256 * (h + 1)].astype(BF16)
-    g_send = core_copy(2, G.at[other], g_peer)
+    g_send = core_copy(2, G.at[other], lambda s: g_peer)
     g_send.start()
 
     def column_grads(acts, grads):
@@ -312,19 +311,35 @@
         return dot(e, grads[0], TN), dot(o, grads[0], TN), dot(e, grads[1], TN)
 
     own = column_grads(act, G.at[c])
-    lx = Exchange("x", X, x, lambda p: LG.at[z, x], lambda s: LG.at[z, s], (lx_s, lx_r))
-    lz = Exchange("z", Z, z, lambda p: LG.at[z], lambda s: LG.at[s], (lz_s, lz_r))
-    act_send.wait_recv()
-    g_send.wait_recv()
+    lx = Exchange("x", X, x, lambda p: LG.at[:, x, c], lambda s: LG.at[:, s, c], (lx_s, lx_r))
+    lc = core_copy(3, LG.at[:, :, c], lambda s: LG.at[:, :, s])
+    act_send.wait_all_recv()
+    g_send.wait_all_recv()
     peers = column_grads(act_peer, g_peer)
     total = jnp.concatenate([a + b for a, b in zip(own, peers)], axis=0)
     DA[...] = total[:, :128].reshape(Y, RY, 128)
-    DB[...] = total[:, 128:].reshape(Y, Z, RZ, 128)
-    ya = Exchange("y", Y, y, lambda p: DA.at[p], lambda s: RA.at[s], (a_s, a_r))
-    zb = Exchange("z", Z, z, lambda p: DB.at[:, p], lambda s: RB.at[s], (b_s, b_r))
+    DB[...] = total[:, 128:].reshape(Y, Z, RZ, 128).transpose(1, 0, 2, 3).reshape(Z, Y * RZ, 128)
+    for full, coded in ((DA, QA), (DB, QB)):
+        values = full[...]
+        n, height, width = values.shape
+        top = jnp.max(jnp.abs(values).reshape(n * height, width), axis=0, keepdims=True)
+        power = jnp.ceil(jnp.log(jnp.maximum(top, 1e-30)) * LOG2E + 0.01) - 15.0
+        ratio = jnp.exp(power * -LN2)
+        coded[:, :height] = jnp.round(values * ratio[None]).astype(jnp.int32).astype(jnp.int16)
+        code = jnp.broadcast_to(power, (16, width)).astype(jnp.int32).astype(jnp.int16)
+        for k in range(n):
+            coded[k, height:] = code
+
+    def decoded(slot):
+        height = slot.shape[0] - 16
+        power = slot[height:, :].astype(jnp.int32).astype(F32)[0:1]
+        return slot[:height, :].astype(jnp.int32).astype(F32) * jnp.exp(power * LN2)
+
+    ya = Exchange("y", Y, y, lambda p: QA.at[p], lambda s: RA.at[s], (a_s, a_r))
+    zb = Exchange("z", Z, z, lambda p: QB.at[p], lambda s: RB.at[s], (b_s, b_r))
     ya.start()
     zb.start()
-    lc_recv.wait_recv()
+    lz.wait_all_recv()
     lx.start()
 
     def whole_grad(k):
@@ -348,7 +363,7 @@
         gpm[at, :] = mid
         return gain_sum + fold8(du * normed), shift_sum + fold8(du)
 
-    gain_sum1, shift_sum1 = lax.fori_loop(0, chunks, backward_chunk, (zero, zero))
+    gain_sum1, shift_sum1 = lax.fori_loop(0, chunks, backward_chunk, (zero, zero), unroll=2)
     taps = dot(xcol[...], gph[...], TN) + dot(xcol[...], gpm[...], TN)
     ri = lax.broadcasted_iota(jnp.int32, (8, C), 0)
     li = lax.broadcasted_iota(jnp.int32, (8, C), 1)
@@ -370,28 +385,28 @@
     ]
     for i, group in enumerate(groups):
         for j in range(4):
-            S[4 * i + j] = group[:, 128 * j : 128 * (j + 1)]
-    sc = core_copy(4, S, S_peer)
+            S[i // 2, 4 * (i % 2) + j] = group[:, 128 * j : 128 * (j + 1)]
+    sc = core_copy(4, S.at[other], lambda s: S_peer)
     sc.start()
     lx.wait_all_recv()
-    lz.start()
-    sc.wait_recv()
-    S1[...] = (S[...] + S_peer[...]).reshape(Y, per_y, 8, 128)
+    lc.start()
+    sc.wait_all_recv()
+    S1[...] = (S[c] + S_peer[...]).reshape(Y, per_y, 8, 128)
     sy = Exchange("y", Y, y, lambda p: S1.at[p], lambda s: SY.at[s], (sy_s, sy_r))
     sy.start()
 
     total = DA[y]
     for r in range(1, Y):
         ya.wait_recv(r)
-        total = total + RA[ya.sender(r)]
+        total = total + decoded(RA.at[ya.sender(r)])
     A1[...] = total.reshape(Z, RZ, 128)
     za = Exchange("z", Z, z, lambda p: A1.at[p], lambda s: RA2.at[s], (a2_s, a2_r))
     za.start()
-    total = DB[:, z]
+    total = DB[z]
     for r in range(1, Z):
         zb.wait_recv(r)
-        total = total + RB[zb.sender(r)]
-    B1[...] = total
+        total = total + decoded(RB.at[zb.sender(r)])
+    B1[...] = total.reshape(Y, RZ, 128)
     yb = Exchange("y", Y, y, lambda p: B1.at[p], lambda s: RB2.at[s], (b2_s, b2_r))
     yb.start()
     sy.wait_all_recv()
@@ -442,22 +457,33 @@
     sa = Exchange("y", Y, y, lambda p: SA.at[y], lambda s: SA.at[s], (sa_s, sa_r))
     sa.start()
 
-    lz.wait_all_recv()
+    lc.wait_all_recv()
     logs = LG[...].reshape(readers, 128)
     picked = sum(dot(pick[...], part, TN) for part in split3(logs))
     lv_ref[...] = picked[:8, : lv_ref.shape[1]]
 
     zg.wait_all_recv()
-    fin_send = core_copy(5, gw2_ref.at[:, half], gw2_ref.at[:, half])
-    fin_recv = core_copy(5, gw2_ref.at[:, other_half], gw2_ref.at[:, other_half])
-    fin_send.start()
+    fin = core_copy(5, gw2_ref.at[:, half], lambda s: gw2_ref.at[:, half_of(s)])
+    fin.start()
 
     sa.wait_all_recv()
-    done = SA[...].reshape(TILES, 8, 128)
-
+    small_ref[c] = SA[...].reshape(TILES // 2, 8, 128)
+    sf = core_copy(6, small_ref.at[c], lambda s: small_ref.at[s])
+    sf.start()
+    sf.wait_all_recv()
+    fin.wait_all_recv()
+
+    waiting = [wy, tc, tx, tz, act_send, g_send, lc, lx, lz, ya, zb, za, yb, xs, zg, sc, sy, sz, sx, sa, sf, fin]
+    for e in waiting + wxs + wcs:
+        e.wait_sends()
+
+
+def write_kernel(lv_in, gw2_in, small, lv_ref, loss_ref, gw2_ref, gw1_ref, gg1_ref, gs1_ref, gg2_ref, gs2_ref):
     def wide(i):
-        return jnp.concatenate([done[4 * i + j] for j in range(4)], axis=1)
-
+        return jnp.concatenate([small[i // 2, 4 * (i % 2) + j] for j in range(4)], axis=1)
+
+    lv_ref[...] = lv_in[...]
+    gw2_ref[...] = gw2_in[...]
     gw1_ref[0:5] = wide(0)[0:5]
     gw1_ref[5:10] = wide(1)[0:5]
     norms = wide(2)
@@ -466,75 +492,64 @@
     gg2_ref[...] = norms[2:3]
     gs2_ref[...] = norms[3:4]
     loss_ref[...] = norms[4:5, 0:1] / norms[4:5, 1:2]
-    fin_recv.wait_recv()
-
-    for e in (wy, tx, tz, lx, lz, ya, zb, za, yb, xs, zg, sy, sz, sx, sa):
-        e.wait_sends()
-    for r in range(1, Y):
-        slot = wy.sender(r)
-        wx(r, slot).wait_sends()
-        wc_send(r, slot).wait_send()
-    for copy in (tc_send, act_send, g_send, lc_send, sc, fin_send):
-        copy.wait_send()
 
 
 def per_device(sizes, waveform, lengths, owner_of, targets, first_weight, first_gain, first_shift,
                second_weight, second_gain, second_shift):
     Z, X, Y = sizes
     row_total, later = targets.shape
-    valid = ((lengths - 10) // 5 - 2) // 2 + 1
-    block = jnp.concatenate(
-        [
-            targets,
-            owner_of.astype(F32)[:, None],
-            valid.astype(F32)[:, None],
-            jnp.zeros((row_total, 128 - later - 2), F32),
-        ],
-        axis=1,
-    )
     RY = second_weight.shape[0]
     RZ = RY // Z
     rows = 320
     dma = pltpu.SemaphoreType.DMA
     vm = pltpu.VMEM
-    per_y = TILES // Y
+    per_y = TILES // 2 // Y
     scratch = [
-        vm((Y, RY, C), BF16), vm((Z, X, 2, 8, 128), F32), vm((Z, X, 2, 8, 128), F32),
+        vm((Y, RY, C), BF16), vm((Z, X, 2, 8, 128), F32), vm((Z, X, 2, 8, 128), F32), vm((8, 128), F32),
         vm((8, 512), F32), vm((128, C), F32), vm((2 * rows, 128), BF16),
         vm((2 * rows, C), F32), vm((2 * rows, C), F32), vm((2 * rows, 128), F32),
         vm((2 * rows, C), BF16), vm((2 * rows, C), BF16), vm((rows, C), F32),
         vm((8, 128), F32), vm((8, 128), F32), vm((rows, C), F32),
         vm((2, 2, rows, 256), BF16), vm((2, rows, 256), BF16),
-        vm((Y, RY, 128), F32), vm((Y, Z, RZ, 128), F32), vm((Y, RY, 128), F32), vm((Z, Y, RZ, 128), F32),
+        vm((Y, RY, 128), F32), vm((Z, Y * RZ, 128), F32),
+        vm((Y, RY + 16, 128), jnp.int16), vm((Z, Y * RZ + 16, 128), jnp.int16),
+        vm((Y, RY + 16, 128), jnp.int16), vm((Z, Y * RZ + 16, 128), jnp.int16),
         vm((Z, RZ, 128), F32), vm((Y, RZ, 128), F32), vm((Z, RZ, 128), F32), vm((Y, RZ, 128), F32),
         vm((X, RZ, 256), F32), vm((2 * rows, C), F32), vm((2 * rows, C), BF16), vm((2 * rows, C), BF16),
-        vm((TILES, 8, 128), F32), vm((TILES, 8, 128), F32), vm((Y, per_y, 8, 128), F32),
+        vm((2, TILES // 2, 8, 128), F32), vm((TILES // 2, 8, 128), F32), vm((Y, per_y, 8, 128), F32),
         vm((Y, per_y, 8, 128), F32), vm((Z, per_y, 8, 128), F32), vm((X, per_y, 8, 128), F32),
         vm((Y, per_y, 8, 128), F32), vm((Z * X * 2 * 8, 128), BF16),
-        dma((Y,)), dma((Y,)), dma((Y, X)), dma((Y, X)), dma((Y,)), dma((Y,)),
+        dma((Y,)), dma((Y,)), dma((Y, X)), dma((Y, X)), dma((Y, 2)), dma((Y, 2)),
         dma((X,)), dma((X,)), dma((Z,)), dma((Z,)), dma((X,)), dma((X,)), dma((Z,)), dma((Z,)),
         dma((Y,)), dma((Y,)), dma((Z,)), dma((Z,)), dma((Z,)), dma((Z,)), dma((Y,)), dma((Y,)),
         dma((X,)), dma((X,)), dma((Z,)), dma((Z,)),
         dma((Y,)), dma((Y,)), dma((Z,)), dma((Z,)), dma((X,)), dma((X,)), dma((Y,)), dma((Y,)),
-        dma((8,)), dma((8,)),
+        dma((8, 2)), dma((8, 2)),
     ]
     shapes = [
         (row_total, later), (1, 1), (RY, C), (10, C), (1, C), (1, C), (1, C), (1, C),
     ]
     whole = pl.BlockSpec(memory_space=pltpu.VMEM)
-    out = pl.pallas_call(
+    scalars = pl.BlockSpec(memory_space=pltpu.SMEM)
+    sums = pl.pallas_call(
         functools.partial(kernel, sizes),
-        out_shape=[jax.ShapeDtypeStruct(s, F32) for s in shapes],
-        in_specs=[whole] * 8,
-        out_specs=[whole] * len(shapes),
+        out_shape=[jax.ShapeDtypeStruct(s, F32) for s in (shapes[0], shapes[2], (2, TILES // 2, 8, 128))],
+        in_specs=[whole, whole, scalars, scalars] + [whole] * 6,
+        out_specs=[whole] * 3,
         scratch_shapes=scratch,
         compiler_params=pltpu.CompilerParams(
             collective_id=0, has_side_effects=True, vmem_limit_bytes=56 * 2**20
         ),
     )(
-        waveform, block, first_weight, first_gain[None], first_shift[None], second_weight,
-        second_gain[None], second_shift[None],
+        waveform, targets, owner_of, lengths, first_weight, first_gain[None], first_shift[None],
+        second_weight, second_gain[None], second_shift[None],
     )
+    out = pl.pallas_call(
+        write_kernel,
+        out_shape=[jax.ShapeDtypeStruct(s, F32) for s in shapes],
+        in_specs=[whole] * 3,
+        out_specs=[whole] * len(shapes),
+    )(*sums)
     lv, loss, gw2, gw1, gg1, gs1, gg2, gs2 = out
     return lv, loss[0, 0], gw2, gw1, gg1[0], gs1[0], gg2[0], gs2[0]
 

time: 96.9 us -> 75 us (0.77)
  Pallas kernels: 85.1 us -> 74.2 us
  local copies, waits for them, and re-layouts: 8.32 us -> 0 us
  between operations: 2.43 us -> 0.64 us
    pallas_call x1, Pallas kernels: 85.1 us -> 72.4 us  [per_device(): pl.pallas_call(functools.partial(kernel, sizes), out_shape=[jax.ShapeDtyp...]
    unnamed x25 -> x0, local copies, waits for them, and re-layouts: 8.08 us -> none
    pallas_call x0 -> x1, Pallas kernels: none -> 1.83 us  [per_device(): pl.pallas_call(write_kernel, out_shape=[jax.ShapeDtypeStruct(s, F32) for...]
where the time goes in v2:
time: 75 us; the launch traced here: 74.9 us
  Pallas kernels  74.2 us (99%)
    pallas_call x1, Pallas kernels, per_device(): pl.pallas_call(functools.partial(kernel, sizes), out_shape=[jax.ShapeDtyp...  72.4 us
    pallas_call x1, Pallas kernels, per_device(): pl.pallas_call(write_kernel, out_shape=[jax.ShapeDtypeStruct(s, F32) for...  1.83 us

profile of v2, /device:TPU:1, one launch (start us, length us, event | category | flops | bytes accessed | tf_op | source)
XLA Modules:
  0.0 74.9 jit_solution(16279305196597987336)
XLA Ops:
  0.6 72.4 %shard_map.161 = (f32[8,39]{1,0:T(8,128)}, f32[192,512]{1,0:T(8,128)}, f32[2,8,8,128]{3,2,1,0:T(8,128)}) custom-call(f32[8,400]{1,0:T(8,128)} %refs_0_.1, f32[8,39]{1,0:T(8,128)} %refs_1_.1, s32[8]{0:T(128)} %refs_2_.1, s32[8]{0:T(128)} %refs_3_.1, f32[10,512]{1,0:T(8,128)} %refs_4_.1, f32[1,512]{1,0:T(1,128)} %bitcast.9, f32[1,512]{1,0:T(1,128)} %bitcast.10, ...), custom_call_target="tpu_custom_call" | custom-call | tf_op jit(solution)/shard_map/pallas_call | solution.py:534
  73.0 1.8 %shard_map.162 = (f32[8,39]{1,0:T(8,128)}, f32[1,1]{1,0:T(1,128)}, f32[192,512]{1,0:T(8,128)}, f32[10,512]{1,0:T(8,128)}, f32[1,512]{1,0:T(1,128)}, /*index=5*/f...) custom-call(f32[8,39]{1,0:T(8,128)} %get-tuple-element.19.lv_in, f32[192,512]{1,0:T(8,128)} %get-tuple-element.20.gw2_in, ...), custom_call_target="tpu_custom_call" | custom-call | tf_op jit(solution)/shard_map/pallas_call | solution.py:547

commit v3 on v2

--- a/solution.py
+++ b/solution.py
@@ -41,7 +41,7 @@
         )
 
     def start(self):
-        for r in range(1, self.size):
+        for r in sorted(range(1, self.size), key=lambda r: -min(r, self.size - r)):
             self._copy(r, self.me, lax.rem(self.me + r, self.size)).start()
 
     def sender(self, r):
@@ -98,13 +98,15 @@
      lv_ref, gw2_ref, small_ref,
      W, TG, LG, blk, wpad, wconv, xcol, xh, dg, rs, act, act_peer, v, tsel, vmask, gf, G, g_peer,
      DA, DB, QA, QB, RA, RB, A1, B1, RA2, RB2, XR, dact, gph, gpm, S, S_peer, SY, S1, SZ, SX, SA, pick,
-     w_sy, w_ry, w_sx, w_rx, w_sc, w_rc, tx_s, tx_r, tz_s, tz_r, lx_s, lx_r, lz_s, lz_r,
+     w_sy, w_ry, w_sd, w_rd, w_sx, w_rx, w_sc, w_rc, tx_s, tx_r, tz_s, tz_r, lx_s, lx_r, lz_s, lz_r,
      a_s, a_r, b_s, b_r, a2_s, a2_r, b2_s, b2_r, x_s, x_r, z_s, z_r,
      sy_s, sy_r, sz_s, sz_r, sx_s, sx_r, sa_s, sa_r, c_s, c_r) = refs
     z, x, c, y = (lax.axis_index(AXES[k]) for k in "zxcy")
     other = 1 - c
     RY = W.shape[1]
-    RX = RY // X
+    routed = RY // 2
+    halves = X // 2
+    RX = routed // halves
     RZ = RY // Z
     rows = 8 * 40
     per_y = TILES // 2 // Y
@@ -134,20 +136,27 @@
     blk[...] = numbers.astype(F32)
     blk[:, : tgt_ref.shape[1]] = tgt_ref[...]
     TG[z, x, c] = blk[...]
-    quarter = pl.ds(pl.multiple_of(x * RX, RX), RX)
-
-    def quarter_of(k):
-        return pl.ds(pl.multiple_of(k * RX, RX), RX)
+
+    def part_rows(k):
+        return pl.ds(pl.multiple_of(k % halves * RX, 16), RX)
+
+    def part_lanes(k):
+        return pl.ds(pl.multiple_of(c * 256 + k // halves * 128, 128), 128)
 
     pl.semaphore_wait(barrier, 1 + (X - 1) + (Y - 1) + (Z - 1))
 
-    wy = Exchange("y", Y, y, lambda p: W.at[y, quarter, half], lambda s: W.at[s, quarter, half], (w_sy, w_ry))
+    wy = Exchange(
+        "y", Y, y, lambda p: W.at[y, part_rows(x), part_lanes(x)],
+        lambda s: W.at[s, part_rows(x), part_lanes(x)], (w_sy, w_ry),
+    )
     wy.start()
+    rest = pl.ds(routed, RY - routed)
+    wd = Exchange("y", Y, y, lambda p: W.at[y, rest, half], lambda s: W.at[s, rest, half], (w_sd, w_rd))
 
     def wx(k, slot):
         return Exchange(
-            "x", X, x, lambda p: W.at[slot, quarter, half],
-            lambda s: W.at[slot, quarter_of(s), half], (w_sx.at[k], w_rx.at[k]),
+            "x", X, x, lambda p: W.at[slot, part_rows(x), part_lanes(x)],
+            lambda s: W.at[slot, part_rows(s), part_lanes(s)], (w_sx.at[k], w_rx.at[k]),
         )
 
     def half_of(k):
@@ -199,6 +208,7 @@
         wconv[base + 16 : base + 21] = fw_mid[taps]
     xh[...] = dot(xcol[...], wconv[...].astype(BF16))
 
+    wd.start()
     g1, s1 = g1_ref[...], s1_ref[...]
 
     def forward_chunk(i, carry):
@@ -215,19 +225,24 @@
         return carry
 
     chunks = 2 * rows // CHUNK
-    lax.fori_loop(0, chunks // 2, forward_chunk, 0, unroll=2)
-    tz.wait_all_recv()
-    tx.start()
-    for r in range(1, Y):
-        wy.wait_recv(r)
-        wxs[r - 1].start()
-    lax.fori_loop(chunks // 2, chunks, forward_chunk, 0, unroll=2)
+    near_first = sorted(range(1, Y), key=lambda r: min(r, Y - r))
+    steps = 4
+    for k in range(steps):
+        for r in near_first[k * 2 : (k + 1) * 2 if k < 2 else Y] if k < 3 else ():
+            wy.wait_recv(r)
+            wxs[r - 1].start()
+        if k == 1:
+            tz.wait_all_recv()
+            tx.start()
+        if k == 3:
+            tx.wait_all_recv()
+            tc.start()
+        lax.fori_loop(chunks * k // steps, chunks * (k + 1) // steps, forward_chunk, 0, unroll=True)
     act_send = core_copy(1, act, lambda s: act_peer)
     act_send.start()
-    tx.wait_all_recv()
-    tc.start()
-    for r in range(1, Y):
+    for r in near_first:
         wxs[r - 1].wait_all_recv()
+        wd.wait_recv(r)
         wcs[r - 1].start()
 
     tc.wait_all_recv()
@@ -295,7 +310,7 @@
 
     zero = jnp.zeros((8, C), F32)
     column = jnp.zeros((40, 1), F32)
-    gain_sum2, shift_sum2, misfit_sum, count = lax.fori_loop(0, 8, head_row, (zero, zero, column, column), unroll=2)
+    gain_sum2, shift_sum2, misfit_sum, count = lax.fori_loop(0, 8, head_row, (zero, zero, column, column), unroll=4)
     lz = Exchange("z", Z, z, lambda p: LG.at[z, x, c], lambda s: LG.at[s, x, c], (lz_s, lz_r))
     lz.start()
     grad = gf[...]
@@ -473,7 +488,7 @@
     sf.wait_all_recv()
     fin.wait_all_recv()
 
-    waiting = [wy, tc, tx, tz, act_send, g_send, lc, lx, lz, ya, zb, za, yb, xs, zg, sc, sy, sz, sx, sa, sf, fin]
+    waiting = [wy, wd, tc, tx, tz, act_send, g_send, lc, lx, lz, ya, zb, za, yb, xs, zg, sc, sy, sz, sx, sa, sf, fin]
     for e in waiting + wxs + wcs:
         e.wait_sends()
 
@@ -519,7 +534,7 @@
         vm((2, TILES // 2, 8, 128), F32), vm((TILES // 2, 8, 128), F32), vm((Y, per_y, 8, 128), F32),
         vm((Y, per_y, 8, 128), F32), vm((Z, per_y, 8, 128), F32), vm((X, per_y, 8, 128), F32),
         vm((Y, per_y, 8, 128), F32), vm((Z * X * 2 * 8, 128), BF16),
-        dma((Y,)), dma((Y,)), dma((Y, X)), dma((Y, X)), dma((Y, 2)), dma((Y, 2)),
+        dma((Y,)), dma((Y,)), dma((Y,)), dma((Y,)), dma((Y, X)), dma((Y, X)), dma((Y, 2)), dma((Y, 2)),
         dma((X,)), dma((X,)), dma((Z,)), dma((Z,)), dma((X,)), dma((X,)), dma((Z,)), dma((Z,)),
         dma((Y,)), dma((Y,)), dma((Z,)), dma((Z,)), dma((Z,)), dma((Z,)), dma((Y,)), dma((Y,)),
         dma((X,)), dma((X,)), dma((Z,)), dma((Z,)),

time: 75 us -> 70.5 us (0.940)
  Pallas kernels: 74.2 us -> 69.7 us
    pallas_call x1, Pallas kernels: 72.4 us -> 67.9 us  [per_device(): pl.pallas_call(functools.partial(kernel, sizes), out_shape=[jax.ShapeDtyp...]
where the time goes in v3:
time: 70.5 us; the launch traced here: 70.4 us
  Pallas kernels  69.7 us (99%)
    pallas_call x1, Pallas kernels, per_device(): pl.pallas_call(functools.partial(kernel, sizes), out_shape=[jax.ShapeDtyp...  67.9 us
    pallas_call x1, Pallas kernels, per_device(): pl.pallas_call(write_kernel, out_shape=[jax.ShapeDtypeStruct(s, F32) for...  1.83 us

profile of v3, /device:TPU:1, one launch (start us, length us, event | category | flops | bytes accessed | tf_op | source)
XLA Modules:
  0.0 70.4 jit_solution(17791597636256060904)
XLA Ops:
  0.6 67.9 %shard_map.161 = (f32[8,39]{1,0:T(8,128)}, f32[192,512]{1,0:T(8,128)}, f32[2,8,8,128]{3,2,1,0:T(8,128)}) custom-call(f32[8,400]{1,0:T(8,128)} %refs_0_.1, f32[8,39]{1,0:T(8,128)} %refs_1_.1, s32[8]{0:T(128)} %refs_2_.1, s32[8]{0:T(128)} %refs_3_.1, f32[10,512]{1,0:T(8,128)} %refs_4_.1, f32[1,512]{1,0:T(1,128)} %bitcast.9, f32[1,512]{1,0:T(1,128)} %bitcast.10, ...), custom_call_target="tpu_custom_call" | custom-call | tf_op jit(solution)/shard_map/pallas_call | solution.py:549
  68.5 1.8 %shard_map.162 = (f32[8,39]{1,0:T(8,128)}, f32[1,1]{1,0:T(1,128)}, f32[192,512]{1,0:T(8,128)}, f32[10,512]{1,0:T(8,128)}, f32[1,512]{1,0:T(1,128)}, /*index=5*/f...) custom-call(f32[8,39]{1,0:T(8,128)} %get-tuple-element.19.lv_in, f32[192,512]{1,0:T(8,128)} %get-tuple-element.20.gw2_in, ...), custom_call_target="tpu_custom_call" | custom-call | tf_op jit(solution)/shard_map/pallas_call | solution.py:562

commit v4 on v3

--- a/solution.py
+++ b/solution.py
@@ -88,6 +88,10 @@
     return u * cdf, cdf + u * (e * 0.3989422804014327)
 
 
+def power_of(top):
+    return jnp.ceil(jnp.log(jnp.maximum(top, 1e-30)) * LOG2E + 0.01) - 15.0
+
+
 def fold8(v):
     return v.reshape(v.shape[0] // 8, 8, v.shape[1]).sum(axis=0)
 
@@ -97,7 +101,7 @@
     (wave_ref, tgt_ref, own_ref, len_ref, fw_ref, g1_ref, s1_ref, w_ref, g2_ref, s2_ref,
      lv_ref, gw2_ref, small_ref,
      W, TG, LG, blk, wpad, wconv, xcol, xh, dg, rs, act, act_peer, v, tsel, vmask, gf, G, g_peer,
-     DA, DB, QA, QB, RA, RB, A1, B1, RA2, RB2, XR, dact, gph, gpm, S, S_peer, SY, S1, SZ, SX, SA, pick,
+     DA, DB, QA, QB, RA, RB, A1, B1, RA2, RB2, XR, dact, gph, gpm, S, S_peer, SY, S1, SZ, SX, SA, pick, FQ,
      w_sy, w_ry, w_sd, w_rd, w_sx, w_rx, w_sc, w_rc, tx_s, tx_r, tz_s, tz_r, lx_s, lx_r, lz_s, lz_r,
      a_s, a_r, b_s, b_r, a2_s, a2_r, b2_s, b2_r, x_s, x_r, z_s, z_r,
      sy_s, sy_r, sz_s, sz_r, sx_s, sx_r, sa_s, sa_r, c_s, c_r) = refs
@@ -310,7 +314,7 @@
 
     zero = jnp.zeros((8, C), F32)
     column = jnp.zeros((40, 1), F32)
-    gain_sum2, shift_sum2, misfit_sum, count = lax.fori_loop(0, 8, head_row, (zero, zero, column, column), unroll=4)
+    gain_sum2, shift_sum2, misfit_sum, count = lax.fori_loop(0, 8, head_row, (zero, zero, column, column), unroll=8)
     lz = Exchange("z", Z, z, lambda p: LG.at[z, x, c], lambda s: LG.at[s, x, c], (lz_s, lz_r))
     lz.start()
     grad = gf[...]
@@ -334,11 +338,11 @@
     total = jnp.concatenate([a + b for a, b in zip(own, peers)], axis=0)
     DA[...] = total[:, :128].reshape(Y, RY, 128)
     DB[...] = total[:, 128:].reshape(Y, Z, RZ, 128).transpose(1, 0, 2, 3).reshape(Z, Y * RZ, 128)
-    for full, coded in ((DA, QA), (DB, QB)):
+    def encode(full, coded):
         values = full[...]
         n, height, width = values.shape
         top = jnp.max(jnp.abs(values).reshape(n * height, width), axis=0, keepdims=True)
-        power = jnp.ceil(jnp.log(jnp.maximum(top, 1e-30)) * LOG2E + 0.01) - 15.0
+        power = power_of(top)
         ratio = jnp.exp(power * -LN2)
         coded[:, :height] = jnp.round(values * ratio[None]).astype(jnp.int32).astype(jnp.int16)
         code = jnp.broadcast_to(power, (16, width)).astype(jnp.int32).astype(jnp.int16)
@@ -352,7 +356,9 @@
 
     ya = Exchange("y", Y, y, lambda p: QA.at[p], lambda s: RA.at[s], (a_s, a_r))
     zb = Exchange("z", Z, z, lambda p: QB.at[p], lambda s: RB.at[s], (b_s, b_r))
+    encode(DA, QA)
     ya.start()
+    encode(DB, QB)
     zb.start()
     lz.wait_all_recv()
     lx.start()
@@ -452,17 +458,17 @@
     sx = Exchange("x", X, x, lambda p: SX.at[x], lambda s: SX.at[s], (sx_s, sx_r))
     sx.start()
 
-    def rows_of(k):
-        return pl.ds(pl.multiple_of(k * RZ, 8), RZ)
-
     xs.wait_all_recv()
     total = XR[0]
     for k in range(1, X):
         total = total + XR[k]
-    gw2_ref[rows_of(z), half] = total
-    zg = Exchange(
-        "z", Z, z, lambda p: gw2_ref.at[rows_of(z), half], lambda s: gw2_ref.at[rows_of(s), half], (z_s, z_r)
-    )
+    power = power_of(jnp.max(jnp.abs(total), axis=0, keepdims=True))
+    spare = FQ.shape[2] - RZ
+    codes = jnp.concatenate(
+        [jnp.round(total * jnp.exp(power * -LN2)), jnp.broadcast_to(power, (spare, 256))], axis=0
+    )
+    FQ[c, z] = codes.astype(jnp.int32).astype(jnp.int16)
+    zg = Exchange("z", Z, z, lambda p: FQ.at[c, z], lambda s: FQ.at[c, s], (z_s, z_r))
     zg.start()
     sx.wait_all_recv()
     total = SX[0]
@@ -478,7 +484,7 @@
     lv_ref[...] = picked[:8, : lv_ref.shape[1]]
 
     zg.wait_all_recv()
-    fin = core_copy(5, gw2_ref.at[:, half], lambda s: gw2_ref.at[:, half_of(s)])
+    fin = core_copy(5, FQ.at[c], lambda s: FQ.at[s])
     fin.start()
 
     sa.wait_all_recv()
@@ -487,6 +493,12 @@
     sf.start()
     sf.wait_all_recv()
     fin.wait_all_recv()
+    for h in range(2):
+        for k in range(Z):
+            piece = FQ[h, k].astype(jnp.int32).astype(F32)
+            gw2_ref[k * RZ : (k + 1) * RZ, 256 * h : 256 * (h + 1)] = piece[:RZ] * jnp.exp(
+                piece[RZ : RZ + 1] * LN2
+            )
 
     waiting = [wy, wd, tc, tx, tz, act_send, g_send, lc, lx, lz, ya, zb, za, yb, xs, zg, sc, sy, sz, sx, sa, sf, fin]
     for e in waiting + wxs + wcs:
@@ -534,6 +546,7 @@
         vm((2, TILES // 2, 8, 128), F32), vm((TILES // 2, 8, 128), F32), vm((Y, per_y, 8, 128), F32),
         vm((Y, per_y, 8, 128), F32), vm((Z, per_y, 8, 128), F32), vm((X, per_y, 8, 128), F32),
         vm((Y, per_y, 8, 128), F32), vm((Z * X * 2 * 8, 128), BF16),
+        vm((2, Z, RZ + (8 if RZ % 16 else 16), 256), jnp.int16),
         dma((Y,)), dma((Y,)), dma((Y,)), dma((Y,)), dma((Y, X)), dma((Y, X)), dma((Y, 2)), dma((Y, 2)),
         dma((X,)), dma((X,)), dma((Z,)), dma((Z,)), dma((X,)), dma((X,)), dma((Z,)), dma((Z,)),
         dma((Y,)), dma((Y,)), dma((Z,)), dma((Z,)), dma((Z,)), dma((Z,)), dma((Y,)), dma((Y,)),

time: 70.5 us -> 69.2 us (0.982)
  Pallas kernels: 69.7 us -> 68.4 us
    pallas_call x1, Pallas kernels: 67.9 us -> 66.6 us  [per_device(): pl.pallas_call(functools.partial(kernel, sizes), out_shape=[jax.ShapeDtyp...]
where the time goes in v4:
time: 69.2 us; the launch traced here: 69.1 us
  Pallas kernels  68.4 us (99%)
    pallas_call x1, Pallas kernels, per_device(): pl.pallas_call(functools.partial(kernel, sizes), out_shape=[jax.ShapeDtyp...  66.6 us
    pallas_call x1, Pallas kernels, per_device(): pl.pallas_call(write_kernel, out_shape=[jax.ShapeDtypeStruct(s, F32) for...  1.83 us

profile of v4, /device:TPU:1, one launch (start us, length us, event | category | flops | bytes accessed | tf_op | source)
XLA Modules:
  0.0 69.1 jit_solution(3827923444467562003)
XLA Ops:
  0.6 66.6 %shard_map.161 = (f32[8,39]{1,0:T(8,128)}, f32[192,512]{1,0:T(8,128)}, f32[2,8,8,128]{3,2,1,0:T(8,128)}) custom-call(f32[8,400]{1,0:T(8,128)} %refs_0_.1, f32[8,39]{1,0:T(8,128)} %refs_1_.1, s32[8]{0:T(128)} %refs_2_.1, s32[8]{0:T(128)} %refs_3_.1, f32[10,512]{1,0:T(8,128)} %refs_4_.1, f32[1,512]{1,0:T(1,128)} %bitcast.9, f32[1,512]{1,0:T(1,128)} %bitcast.10, ...), custom_call_target="tpu_custom_call" | custom-call | tf_op jit(solution)/shard_map/pallas_call | solution.py:562
  67.2 1.8 %shard_map.162 = (f32[8,39]{1,0:T(8,128)}, f32[1,1]{1,0:T(1,128)}, f32[192,512]{1,0:T(8,128)}, f32[10,512]{1,0:T(8,128)}, f32[1,512]{1,0:T(1,128)}, /*index=5*/f...) custom-call(f32[8,39]{1,0:T(8,128)} %get-tuple-element.19.lv_in, f32[192,512]{1,0:T(8,128)} %get-tuple-element.20.gw2_in, ...), custom_call_target="tpu_custom_call" | custom-call | tf_op jit(solution)/shard_map/pallas_call | solution.py:575

commit v5 on v4

--- a/solution.py
+++ b/solution.py
@@ -98,8 +98,9 @@
 
 def kernel(sizes, *refs):
     Z, X, Y = sizes
-    (wave_ref, tgt_ref, own_ref, len_ref, fw_ref, g1_ref, s1_ref, w_ref, g2_ref, s2_ref,
+    (wave_in, tgt_in, own_in, len_in, fw_in, g1_in, s1_in, w_in, g2_in, s2_in,
      lv_ref, gw2_ref, small_ref,
+     wave_ref, tgt_ref, own_ref, len_ref, fw_ref, g1_ref, s1_ref, g2_ref, s2_ref, in_s,
      W, TG, LG, blk, wpad, wconv, xcol, xh, dg, rs, act, act_peer, v, tsel, vmask, gf, G, g_peer,
      DA, DB, QA, QB, RA, RB, A1, B1, RA2, RB2, XR, dact, gph, gpm, S, S_peer, SY, S1, SZ, SX, SA, pick, FQ,
      w_sy, w_ry, w_sd, w_rd, w_sx, w_rx, w_sc, w_rc, tx_s, tx_r, tz_s, tz_r, lx_s, lx_r, lz_s, lz_r,
@@ -130,7 +131,19 @@
 
     half = pl.ds(pl.multiple_of(c * 256, 256), 256)
 
-    W[y] = w_ref[...]
+    loads = [
+        pltpu.make_async_copy(source, target, in_s.at[k])
+        for k, (source, target) in enumerate(
+            (
+                (w_in, W.at[y]), (own_in, own_ref), (len_in, len_ref), (tgt_in, tgt_ref), (wave_in, wave_ref),
+                (fw_in, fw_ref), (g1_in, g1_ref), (s1_in, s1_ref), (g2_in, g2_ref), (s2_in, s2_ref),
+            )
+        )
+    ]
+    for load in loads:
+        load.start()
+    for load in loads[:4]:
+        load.wait()
     r8 = lax.broadcasted_iota(jnp.int32, (8, 128), 0)
     l8 = lax.broadcasted_iota(jnp.int32, (8, 128), 1)
     numbers = jnp.zeros((8, 128), jnp.int32)
@@ -179,6 +192,8 @@
     tx = Exchange("x", X, x, lambda p: TG.at[:, x, c], lambda s: TG.at[:, s, c], (tx_s, tx_r))
     tc = core_copy(0, TG.at[:, :, c], lambda s: TG.at[:, :, s])
 
+    for load in loads[4:]:
+        load.wait()
     wpad[...] = jnp.zeros_like(wpad)
     wpad[:, : wave_ref.shape[1]] = wave_ref[...]
     samples = lax.broadcasted_iota(jnp.int32, (512, 128), 0).astype(F32)
@@ -532,6 +547,9 @@
     vm = pltpu.VMEM
     per_y = TILES // 2 // Y
     scratch = [
+        vm(waveform.shape, F32), vm(targets.shape, F32), pltpu.SMEM(owner_of.shape, jnp.int32),
+        pltpu.SMEM(lengths.shape, jnp.int32), vm(first_weight.shape, F32), vm((1, C), F32), vm((1, C), F32),
+        vm((1, C), F32), vm((1, C), F32), dma((10,)),
         vm((Y, RY, C), BF16), vm((Z, X, 2, 8, 128), F32), vm((Z, X, 2, 8, 128), F32), vm((8, 128), F32),
         vm((8, 512), F32), vm((128, C), F32), vm((2 * rows, 128), BF16),
         vm((2 * rows, C), F32), vm((2 * rows, C), F32), vm((2 * rows, 128), F32),
@@ -558,11 +576,10 @@
         (row_total, later), (1, 1), (RY, C), (10, C), (1, C), (1, C), (1, C), (1, C),
     ]
     whole = pl.BlockSpec(memory_space=pltpu.VMEM)
-    scalars = pl.BlockSpec(memory_space=pltpu.SMEM)
     sums = pl.pallas_call(
         functools.partial(kernel, sizes),
         out_shape=[jax.ShapeDtypeStruct(s, F32) for s in (shapes[0], shapes[2], (2, TILES // 2, 8, 128))],
-        in_specs=[whole, whole, scalars, scalars] + [whole] * 6,
+        in_specs=[pl.BlockSpec(memory_space=pl.ANY)] * 10,
         out_specs=[whole] * 3,
         scratch_shapes=scratch,
         compiler_params=pltpu.CompilerParams(

time: 69.2 us -> 68.3 us (0.987)
  Pallas kernels: 68.4 us -> 67.5 us
    pallas_call x1, Pallas kernels: 66.6 us -> 65.7 us  [per_device(): pl.pallas_call(functools.partial(kernel, sizes), out_shape=[jax.ShapeDtyp...]
where the time goes in v5:
time: 68.3 us; the launch traced here: 68.2 us
  Pallas kernels  67.5 us (99%)
    pallas_call x1, Pallas kernels, per_device(): pl.pallas_call(functools.partial(kernel, sizes), out_shape=[jax.ShapeDtyp...  65.7 us
    pallas_call x1, Pallas kernels, per_device(): pl.pallas_call(write_kernel, out_shape=[jax.ShapeDtypeStruct(s, F32) for...  1.83 us

profile of v5, /device:TPU:1, one launch (start us, length us, event | category | flops | bytes accessed | tf_op | source)
XLA Modules:
  0.0 68.2 jit_solution(12923845896189780140)
XLA Ops:
  0.6 65.7 %shard_map.161 = (f32[8,39]{1,0:T(8,128)}, f32[192,512]{1,0:T(8,128)}, f32[2,8,8,128]{3,2,1,0:T(8,128)}) custom-call(f32[8,400]{1,0:T(8,128)} %refs_0_.1, f32[8,39]{1,0:T(8,128)} %refs_1_.1, s32[8]{0:T(128)} %refs_2_.1, s32[8]{0:T(128)} %refs_3_.1, f32[10,512]{1,0:T(8,128)} %refs_4_.1, f32[1,512]{1,0:T(1,128)} %bitcast.9, f32[1,512]{1,0:T(1,128)} %bitcast.10, ...), custom_call_target="tpu_custom_call" | custom-call | tf_op jit(solution)/shard_map/pallas_call | solution.py:579
  66.3 1.8 %shard_map.162 = (f32[8,39]{1,0:T(8,128)}, f32[1,1]{1,0:T(1,128)}, f32[192,512]{1,0:T(8,128)}, f32[10,512]{1,0:T(8,128)}, f32[1,512]{1,0:T(1,128)}, /*index=5*/f...) custom-call(f32[8,39]{1,0:T(8,128)} %get-tuple-element.19.lv_in, f32[192,512]{1,0:T(8,128)} %get-tuple-element.20.gw2_in, ...), custom_call_target="tpu_custom_call" | custom-call | tf_op jit(solution)/shard_map/pallas_call | solution.py:592

commit v6 on v5

--- a/solution.py
+++ b/solution.py
@@ -578,7 +578,7 @@
     whole = pl.BlockSpec(memory_space=pltpu.VMEM)
     sums = pl.pallas_call(
         functools.partial(kernel, sizes),
-        out_shape=[jax.ShapeDtypeStruct(s, F32) for s in (shapes[0], shapes[2], (2, TILES // 2, 8, 128))],
+        out_shape=[vm(s, F32) for s in (shapes[0], shapes[2], (2, TILES // 2, 8, 128))],
         in_specs=[pl.BlockSpec(memory_space=pl.ANY)] * 10,
         out_specs=[whole] * 3,
         scratch_shapes=scratch,
@@ -594,7 +594,7 @@
         out_shape=[jax.ShapeDtypeStruct(s, F32) for s in shapes],
         in_specs=[whole] * 3,
         out_specs=[whole] * len(shapes),
-    )(*sums)
+    )(*[pltpu.with_memory_space_constraint(a, pltpu.VMEM) for a in sums])
     lv, loss, gw2, gw1, gg1, gs1, gg2, gs2 = out
     return lv, loss[0, 0], gw2, gw1, gg1[0], gs1[0], gg2[0], gs2[0]
 

time: 68.3 us -> 66.5 us (0.974)
  Pallas kernels: 67.5 us -> 65.7 us
    pallas_call x1, Pallas kernels: 1.83 us -> 0.83 us  [per_device(): pl.pallas_call(write_kernel, out_shape=[jax.ShapeDtypeStruct(s, F32) for...]
    pallas_call x1, Pallas kernels: 65.7 us -> 64.9 us  [per_device(): pl.pallas_call(functools.partial(kernel, sizes), out_shape=[vm(s, F32) fo...]
where the time goes in v6:
time: 66.5 us; the launch traced here: 66.4 us
  Pallas kernels  65.7 us (99%)
    pallas_call x1, Pallas kernels, per_device(): pl.pallas_call(functools.partial(kernel, sizes), out_shape=[vm(s, F32) fo...  64.9 us

profile of v6, /device:TPU:1, one launch (start us, length us, event | category | flops | bytes accessed | tf_op | source)
XLA Modules:
  0.0 66.4 jit_solution(9998822693023408735)
XLA Ops:
  0.6 64.9 %shard_map.161 = (f32[8,39]{1,0:T(8,128)S(1)}, f32[192,512]{1,0:T(8,128)S(1)}, f32[2,8,8,128]{3,2,1,0:T(8,128)S(1)}) custom-call(f32[8,400]{1,0:T(8,128)} %refs_0_.1, f32[8,39]{1,0:T(8,128)} %refs_1_.1, s32[8]{0:T(128)} %refs_2_.1, s32[8]{0:T(128)} %refs_3_.1, f32[10,512]{1,0:T(8,128)} %refs_4_.1, f32[1,512]{1,0:T(1,128)} %bitcast.9, f32[1,512]{1,0:T(1,128)} %bitcast.10, ...), custom_call_target="tpu_custom_call" | custom-call | tf_op jit(solution)/shard_map/pallas_call | solution.py:579
  65.5 0.8 %shard_map.162 = (f32[8,39]{1,0:T(8,128)}, f32[1,1]{1,0:T(1,128)}, f32[192,512]{1,0:T(8,128)}, f32[10,512]{1,0:T(8,128)}, f32[1,512]{1,0:T(1,128)}, /*index=5*/f...) custom-call(f32[8,39]{1,0:T(8,128)S(1)} %get-tuple-element.19.lv_in, f32[192,512]{1,0:T(8,128)S(1)} %get-tuple-element.20.gw2_in, ...), custom_call_target="tpu_custom_call" | custom-call | tf_op jit(solution)/shard_map/pallas_call | solution.py:592
